TPU v7x, 32 devices: a whole 2x2x4 slice. The times are simulated.
32 devices in a mesh: fsdp: 8 (over z, y), grp: 4 (over x, core).
Axes of the slice: x: 2, y: 2, z: 4, core: 2. Of those that a mesh axis runs over, the one named last changes fastest.
Arguments:
- latents: bfloat16 [2048, 512], P('fsdp'), may hold values from -6 to 6
- queries: bfloat16 [2048, 128, 128], P('fsdp', 'grp')
- grad_out: bfloat16 [2048, 128, 128], P('fsdp', 'grp'), may hold values from -6 to 6
- kv_weight: bfloat16 [4, 32, 512, 256], P('grp', 'fsdp'), may hold values from -0.25 to 0.25
- doc_ids: int32 [2048], replicated, may hold values from 0 to 3, never falling along the last dimension, each value on 1 to 1024 neighbouring positions
- block_lists: int32 [32, 4], replicated, may hold values from 0 to 31, as said below
Outputs:
- grad_queries: bfloat16 [2048, 128, 128], P('fsdp', 'grp')
- grad_latents: float32 [2048, 512], P('fsdp', 'grp')
- grad_weight: float32 [4, 32, 512, 256], P('grp', 'fsdp')
Inputs may be any that keep to these rules, and one draw needn't show every extreme that they name: `block_lists`: row b belongs to query block b; its first entry is b and its 4 entries differ. Take the 4 rows of one run f (rows f * 4 to f * 4 + 3) without their first entries: for every d from 1 to 6 with f - d >= 0, exactly 2 of these entries, counted with repeats, are blocks of run f - d; all other entries are blocks of run f itself.
All inputs are finite; a program needn't handle non-finite values.
Results may differ from a plain program's by a relative error of at most 0.035.
The roundings to bfloat16 on the way count: a program that leaves them out, or rounds other values in their place, can miss the bound.
Values may be sent and summed in bfloat16 or wider, within the bound.
A program may use at most 128 MiB of HBM per device.

v0:
```python
import jax
import jax.numpy as jnp
from jax import lax
from jax.sharding import PartitionSpec as P

BLK = 64
TOPK = 4
DIST = 6


NEG_FILL = -1e30


def passed_along(block, axis, distance):
    devices = range(lax.axis_size(axis))
    route = [(i - distance, i) for i in devices if i - distance in devices]
    return lax.ppermute(block, axis, route)


def head_pass(w_head, q_head, g_head, key_lat, visible, score_scale):
    head_width = q_head.shape[-1]
    block_count = q_head.shape[0]
    expanded = jnp.dot(key_lat, w_head, preferred_element_type=jnp.float32).astype(jnp.bfloat16)
    expanded = expanded.reshape(block_count, -1, 2 * head_width)
    key_rows = expanded[:, :, :head_width]
    value_rows = expanded[:, :, head_width:]
    scores = (
        jnp.einsum("qbd,qkd->qbk", q_head, key_rows, preferred_element_type=jnp.float32)
        * score_scale
    )
    scores = jnp.where(visible, scores, NEG_FILL)
    row_max = jnp.max(scores, axis=-1, keepdims=True)
    exp_scores = jnp.exp(scores - row_max)
    softmax_p = exp_scores / jnp.sum(exp_scores, axis=-1, keepdims=True)
    probs_low = softmax_p.astype(jnp.bfloat16)
    attended = jnp.einsum("qbk,qkd->qbd", probs_low, value_rows, preferred_element_type=jnp.float32)
    delta_rows = jnp.sum(g_head.astype(jnp.float32) * attended, axis=-1, keepdims=True)
    grad_probs = jnp.einsum("qbd,qkd->qbk", g_head, value_rows, preferred_element_type=jnp.float32)
    grad_scores = (softmax_p * (grad_probs - delta_rows)).astype(jnp.bfloat16)
    grad_q = (
        jnp.einsum("qbk,qkd->qbd", grad_scores, key_rows, preferred_element_type=jnp.float32)
        * score_scale
    ).astype(jnp.bfloat16)
    grad_k = (
        jnp.einsum("qbk,qbd->qkd", grad_scores, q_head, preferred_element_type=jnp.float32)
        * score_scale
    ).astype(jnp.bfloat16)
    grad_v = jnp.einsum(
        "qbk,qbd->qkd", probs_low, g_head, preferred_element_type=jnp.float32
    ).astype(jnp.bfloat16)
    grad_kv = jnp.concatenate([grad_k, grad_v], axis=-1).reshape(-1, 2 * head_width)
    lat_part = lax.dot_general(
        grad_kv, w_head, (((1,), (1,)), ((), ())), preferred_element_type=jnp.float32
    )
    grad_w = lax.dot_general(
        key_lat, grad_kv, (((0,), (0,)), ((), ())), preferred_element_type=jnp.float32
    )
    return (grad_q.reshape(-1, head_width), lat_part, grad_w)


def visibility(doc_ids, list_rows, query_start, block_count):
    offsets = jnp.arange(BLK, dtype=jnp.int32)
    key_pos = (list_rows[:, :, None] * BLK + offsets[None, None, :]).reshape(block_count, -1)
    query_pos = (query_start + jnp.arange(block_count * BLK, dtype=jnp.int32)).reshape(
        block_count, BLK
    )
    key_doc = jnp.take(doc_ids, key_pos)
    query_doc = jnp.take(doc_ids, query_pos)
    visible = (key_doc[:, None, :] == query_doc[:, :, None]) & (
        key_pos[:, None, :] <= query_pos[:, :, None]
    )
    return (key_pos, visible)


def earlier_count(flags):
    positions = jnp.arange(flags.shape[0])
    earlier = positions[None, :] < positions[:, None]
    return jnp.sum(flags & earlier, axis=1)


def slot_ranks(owner_ids):
    positions = jnp.arange(owner_ids.shape[0])
    same_owner = owner_ids[None, :] == owner_ids[:, None]
    earlier = positions[None, :] < positions[:, None]
    return jnp.sum(same_owner & earlier, axis=1)


def per_device(latents, queries, grad_out, kv_weight, doc_ids, block_lists):
    device_pos = lax.axis_index("fsdp")
    tok_rows, lat_width = latents.shape
    head_dim = queries.shape[2]
    head_count = queries.shape[1]
    block_count = tok_rows // BLK
    extra_picks = TOPK - 1
    slot_cap = block_count * extra_picks // DIST
    lat_share = lat_width // lax.axis_size("grp")
    score_scale = head_dim ** (-0.5)
    own_lists = lax.dynamic_slice_in_dim(block_lists, device_pos * block_count, block_count, 0)
    remote_ids = own_lists[:, 1:].reshape(-1)
    owner_ids = remote_ids // block_count
    owner_ranks = slot_ranks(owner_ids)
    remote_pool = jnp.where(
        owner_ids == device_pos,
        remote_ids % block_count,
        block_count + (device_pos - owner_ids - 1) * slot_cap + owner_ranks,
    )
    pool_index = jnp.concatenate(
        [
            jnp.arange(block_count, dtype=jnp.int32)[:, None],
            remote_pool.reshape(block_count, extra_picks),
        ],
        axis=1,
    )
    local_blocks = latents.reshape(block_count, BLK, lat_width)
    send_lists = []
    arrived = []
    for distance in range(1, DIST + 1):
        reader_lists = lax.dynamic_slice_in_dim(
            block_lists, (device_pos + distance) * block_count, block_count, 0
        )
        reader_remote = reader_lists[:, 1:].reshape(-1)
        wanted = reader_remote // block_count == device_pos
        reader_ranks = earlier_count(wanted[None, :] & jnp.ones((wanted.shape[0], 1), bool))
        choose_table = wanted[None, :] & (reader_ranks[None, :] == jnp.arange(slot_cap)[:, None])
        send_index = jnp.sum(
            jnp.where(choose_table, (reader_remote % block_count)[None, :], 0), axis=1
        )
        send_lists.append(send_index)
        outgoing = jnp.take(local_blocks, send_index, axis=0)
        arrived.append(passed_along(outgoing, "fsdp", distance))
    fetched = jnp.concatenate(arrived, axis=0)
    block_pool = jnp.concatenate([local_blocks, fetched], axis=0)
    key_lat = jnp.take(block_pool, pool_index.reshape(-1), axis=0).reshape(-1, lat_width)
    key_pos, visible = visibility(doc_ids, own_lists, device_pos * tok_rows, block_count)

    def run_head(head_idx, w_head, grad_q_all, grad_lat):
        q_head = lax.dynamic_index_in_dim(queries, head_idx, 1, False).reshape(
            block_count, BLK, head_dim
        )
        g_head = lax.dynamic_index_in_dim(grad_out, head_idx, 1, False).reshape(
            block_count, BLK, head_dim
        )
        grad_q, lat_part, grad_w = head_pass(w_head, q_head, g_head, key_lat, visible, score_scale)
        grad_q_all = lax.dynamic_update_index_in_dim(grad_q_all, grad_q, head_idx, 1)
        return (grad_q_all, grad_lat + lat_part, grad_w)

    zero_q = jnp.zeros(queries.shape, jnp.bfloat16)
    zero_lat = jnp.zeros(key_lat.shape, jnp.float32)
    zero_w = jnp.zeros((head_count,) + kv_weight.shape[2:], jnp.float32)
    w_piece = lax.all_gather(kv_weight, "fsdp", axis=1, tiled=True)

    def per_head(head_idx, inner_state):
        grad_q_all, grad_lat, grad_w_all = inner_state
        w_head = lax.dynamic_index_in_dim(w_piece[0], head_idx, 0, False)
        grad_q_all, grad_lat, grad_w = run_head(head_idx, w_head, grad_q_all, grad_lat)
        grad_w_all = lax.dynamic_update_index_in_dim(grad_w_all, grad_w, head_idx, 0)
        return (grad_q_all, grad_lat, grad_w_all)

    grad_q_all, grad_lat, grad_w_all = lax.fori_loop(
        0, w_piece.shape[1], per_head, (zero_q, zero_lat, zero_w)
    )
    grad_weight = lax.psum_scatter(
        grad_w_all.astype(jnp.bfloat16), "fsdp", scatter_dimension=0, tiled=True
    ).astype(jnp.float32)[None]
    slot_grads = grad_lat.reshape(block_count, TOPK, BLK, lat_width)
    lat_shares = lax.psum_scatter(slot_grads, "grp", scatter_dimension=3, tiled=True).reshape(
        block_count * TOPK, BLK * lat_share
    )
    flat_pool = pool_index.reshape(-1)
    own_table = (flat_pool[None, :] == jnp.arange(block_count)[:, None]).astype(jnp.float32)
    lat_total = jnp.dot(own_table, lat_shares, precision=lax.Precision.HIGHEST)
    for distance in range(1, DIST + 1):
        slot_ids = block_count + (distance - 1) * slot_cap + jnp.arange(slot_cap)
        pick_table = (flat_pool[None, :] == slot_ids[:, None]).astype(jnp.float32)
        outgoing = jnp.dot(pick_table, lat_shares, precision=lax.Precision.HIGHEST)
        returned = passed_along(outgoing, "fsdp", -distance)
        place_table = (
            send_lists[distance - 1][None, :] == jnp.arange(block_count)[:, None]
        ).astype(jnp.float32)
        lat_total = lat_total + jnp.dot(place_table, returned, precision=lax.Precision.HIGHEST)
    grad_latents = lat_total.reshape(tok_rows, lat_share)
    return (grad_q_all, grad_latents, grad_weight)


def solution(mesh):
    return jax.shard_map(
        per_device,
        mesh=mesh,
        in_specs=(
            P("fsdp", None),
            P("fsdp", "grp", None),
            P("fsdp", "grp", None),
            P("grp", "fsdp", None, None),
            P(),
            P(),
        ),
        out_specs=(P("fsdp", "grp", None), P("fsdp", "grp"), P("grp", "fsdp", None, None)),
        check_vma=False,
    )
```

profile of v0, /device:TPU:0, one launch (start us, length us, event | category | flops | bytes accessed | tf_op | source)
XLA Modules:
  0.0 774.4 jit_solution(2341958369679455685)
XLA Ops:
  11.3 4.9 collective-permute-start
  18.1 3.5 collective-permute-start.1
  22.9 4.4 collective-permute-start.2
  28.3 2.0 collective-permute-start.3
  35.1 6.1 gather_fusion.1
  48.3 3.9 copy.63
  52.1 2.1 copy.65
  58.9 2.8 collective-permute-done.5
  62.3 2.0 gather_fusion
  65.5 90.7 %all-gather.2.cloned.1.call-done = bf16[1,32,512,256]{3,2,0,1:T(8,128)(2,1)} async-done(((bf16[1,4,512,256]{3,2,0,1:T(8,128)(2,1)}), bf16[1,32,512,256]{3,2,0,1:T(8,128)(2,1)}) %all-gather.2.cloned.1.call-update) | async-done | bytes 8388624 | tf_op jit(solution)/shard_map/all_gather | solution.py:150
  156.2 417.9 %while.18 = (s32[]{:T(128)}, bf16[256,32,128]{2,0,1:T(8,128)(2,1)}, f32[1024,512]{1,0:T(8,128)S(1)}, bf16[32,512,256]{2,1,0:T(8,128)(2,1)}, bf16[256,32,128]{2,0...) while((s32[]{:T(128)}, bf16[256,32,128]{2,0,1:T(8,128)(2,1)}, ...), condition=%wide.region_17.19_spmd.clone, body=%wide.region_13.18_spmd.clone.sunk | while | flops 910001152 | bytes 22738324 | solution.py:159
  156.2 1.8 fusion.171
  166.7 1.7 select_add_fusion.2
  169.3 1.8 fusion.171
  182.4 1.8 fusion.171
  192.8 1.7 select_add_fusion.2
  195.4 1.8 fusion.171
  208.5 1.8 fusion.171
  221.6 1.8 fusion.171
  232.0 1.7 select_add_fusion.2
  234.6 1.8 fusion.171
  247.7 1.8 fusion.171
  258.1 1.7 select_add_fusion.2
  260.7 1.8 fusion.171
  273.8 1.8 fusion.171
  286.8 1.8 fusion.171
  299.9 1.8 fusion.171
  310.3 1.7 select_add_fusion.2
  313.0 1.8 fusion.171
  326.0 1.8 fusion.171
  336.4 1.7 select_add_fusion.2
  339.1 1.8 fusion.171
  352.1 1.8 fusion.171
  365.2 1.8 fusion.171
  375.6 1.7 select_add_fusion.2
  378.2 1.8 fusion.171
  391.3 1.8 fusion.171
  401.8 1.7 select_add_fusion.2
  404.4 1.8 fusion.171
  414.8 1.7 select_add_fusion.2
  417.5 1.8 fusion.171
  430.5 1.8 fusion.171
  440.9 1.7 select_add_fusion.2
  443.5 1.8 fusion.171
  454.0 1.7 select_add_fusion.2
  456.6 1.8 fusion.171
  469.6 1.8 fusion.171
  482.7 1.8 fusion.171
  493.2 1.7 select_add_fusion.2
  495.8 1.8 fusion.171
  508.8 1.8 fusion.171
  519.3 1.7 select_add_fusion.2
  521.9 1.8 fusion.171
  532.3 1.7 select_add_fusion.2
  535.0 1.8 fusion.171
  545.4 1.7 select_add_fusion.2
  548.0 1.8 fusion.171
  561.1 1.8 fusion.171
  576.3 4.3 copy.67
  580.5 24.7 %reduce-scatter.3.cloned.1.call-done = f32[4,4,64,128]{3,2,1,0:T(8,128)} async-done(((f32[4,4,64,512]{3,2,1,0:T(8,128)}), f32[4,4,64,128]{3,2,1,0:T(8,128)}) %reduce-scatter.3.cloned.1.call-update) | async-done | bytes 524304 | tf_op jit(solution)/shard_map/reduce_scatter | solution.py:166
  622.2 7.6 collective-permute-done.9
  630.0 5.4 collective-permute-done.10
  637.0 128.2 %reduce-scatter.5.cloned.1.call-done = bf16[4,512,256]{2,1,0:T(8,128)(2,1)} async-done(((bf16[32,512,256]{2,1,0:T(8,128)(2,1)}), bf16[4,512,256]{2,1,0:T(8,128)(2,1)}) %reduce-scatter.5.cloned.1.call-update) | async-done | bytes 1048592 | tf_op jit(solution)/shard_map/reduce_scatter | solution.py:162
  765.2 2.7 bitcast_convert_fusion
  (1207 shorter events, 375.8 us)
Async XLA Ops:
  7.2 27.9 %copy-start = (s32[2048]{0:T(1024)S(1)}, s32[2048]{0:T(1024)}, u32[]{:S(2)}) copy-start(s32[2048]{0:T(1024)} %param.14) | copy-start | bytes 24580
  7.2 15.1 %copy-start.5 = (bf16[256,512]{1,0:T(8,128)(2,1)S(1)}, bf16[256,512]{1,0:T(8,128)(2,1)}, u32[]{:S(2)}) copy-start(bf16[256,512]{1,0:T(8,128)(2,1)} %param.10) | copy-start | bytes 786436
  7.2 149.0 %all-gather.2.cloned.1.call-start = ((), (), s32[]{:S(2)}) async-start(), calls=%async_computation.2 | async-start | bytes 9437184 | tf_op jit(solution)/shard_map/all_gather | solution.py:150
  7.9 597.3 %reduce-scatter.3.cloned.1.call-start = ((), (), s32[]{:S(2)}) async-start(), calls=%async_computation.3 | async-start | bytes 2621440 | tf_op jit(solution)/shard_map/reduce_scatter | solution.py:166
  9.7 6.6 copy-start.16
  11.3 43.0 %collective-permute-start = (bf16[2,64,512]{2,1,0:T(8,128)(2,1)S(1)}, bf16[2,64,512]{2,1,0:T(8,128)(2,1)S(1)}, u32[]{:S(2)}, u32[]{:S(2)}) collective-permute-start(bf16[2,64,512]{2,1,0:T(8,128)(2,1)S(1)} %broadcast_select_fusion.5), channel_id=1, source_target_pairs={{0,4},{4,8},{8,12},{12,16},{16,20},{20,24},{24,28},{1,5},{5,9},{9,... | collective-permute-start | bytes 393224 | tf_op jit(solution)/shard_map/ppermute | solution.py:17
  16.4 24.8 %copy-start.14 = (s32[2]{0:T(128)}, s32[2]{0:T(128)S(1)}, u32[]{:S(2)}) copy-start(s32[2]{0:T(128)S(1)} %fusion.71) | copy-start | bytes 28
  18.1 38.2 %collective-permute-start.1 = (bf16[2,64,512]{2,1,0:T(8,128)(2,1)S(1)}, bf16[2,64,512]{2,1,0:T(8,128)(2,1)S(1)}, u32[]{:S(2)}, u32[]{:S(2)}) collective-permute-start(bf16[2,64,512]{2,1,0:T(8,128)(2,1)S(1)} %broadcast_select_fusion.4), channel_id=1, source_target_pairs={{0,8},{4,12},{8,16},{12,20},{16,24},{20,28},{1,9},{5,13},{9,17},{1... | collective-permute-start | bytes 393224 | tf_op jit(solution)/shard_map/ppermute | solution.py:17
  22.2 19.1 %copy-start.18 = (s32[2]{0:T(128)}, s32[2]{0:T(128)S(1)}, u32[]{:S(2)}) copy-start(s32[2]{0:T(128)S(1)} %fusion.72) | copy-start | bytes 28
  22.9 34.0 %collective-permute-start.2 = (bf16[2,64,512]{2,1,0:T(8,128)(2,1)S(1)}, bf16[2,64,512]{2,1,0:T(8,128)(2,1)S(1)}, u32[]{:S(2)}, u32[]{:S(2)}) collective-permute-start(bf16[2,64,512]{2,1,0:T(8,128)(2,1)S(1)} %broadcast_select_fusion.3), channel_id=1, source_target_pairs={{0,12},{4,16},{8,20},{12,24},{16,28},{1,13},{5,17},{9,21},{13,25},... | collective-permute-start | bytes 393224 | tf_op jit(solution)/shard_map/ppermute | solution.py:17
  27.6 13.7 %copy-start.20 = (s32[2]{0:T(128)}, s32[2]{0:T(128)S(1)}, u32[]{:S(2)}) copy-start(s32[2]{0:T(128)S(1)} %fusion.73) | copy-start | bytes 28
  28.3 29.2 %collective-permute-start.3 = (bf16[2,64,512]{2,1,0:T(8,128)(2,1)S(1)}, bf16[2,64,512]{2,1,0:T(8,128)(2,1)S(1)}, u32[]{:S(2)}, u32[]{:S(2)}) collective-permute-start(bf16[2,64,512]{2,1,0:T(8,128)(2,1)S(1)} %broadcast_select_fusion.2), channel_id=1, source_target_pairs={{0,16},{4,20},{8,24},{12,28},{1,17},{5,21},{9,25},{13,29},{2,18},{... | collective-permute-start | bytes 393224 | tf_op jit(solution)/shard_map/ppermute | solution.py:17
  30.9 10.4 %copy-start.22 = (s32[2]{0:T(128)}, s32[2]{0:T(128)S(1)}, u32[]{:S(2)}) copy-start(s32[2]{0:T(128)S(1)} %fusion.74) | copy-start | bytes 28
  31.6 26.6 %collective-permute-start.4 = (bf16[2,64,512]{2,1,0:T(8,128)(2,1)S(1)}, bf16[2,64,512]{2,1,0:T(8,128)(2,1)S(1)}, u32[]{:S(2)}, u32[]{:S(2)}) collective-permute-start(bf16[2,64,512]{2,1,0:T(8,128)(2,1)S(1)} %broadcast_select_fusion.1), channel_id=1, source_target_pairs={{0,20},{4,24},{8,28},{1,21},{5,25},{9,29},{2,22},{6,26},{10,30},{3... | collective-permute-start | bytes 393224 | tf_op jit(solution)/shard_map/ppermute | solution.py:17
  34.3 9.6 %copy-start.24 = (s32[2]{0:T(128)}, s32[2]{0:T(128)S(1)}, u32[]{:S(2)}) copy-start(s32[2]{0:T(128)S(1)} %fusion.75) | copy-start | bytes 28
  48.3 3.9 copy-start.8
  54.3 10.0 %copy-start.9 = (pred[1024]{0:T(1024)(128)(4,1)S(1)}, pred[1024]{0:T(1024)(128)(4,1)}, u32[]{:S(2)}) copy-start(pred[1024]{0:T(1024)(128)(4,1)} %broadcast_in_dim.199) | copy-start | bytes 3076
  54.3 7.4 collective-permute-start.5
  62.3 93.9 %copy-start.10 = (s32[4,256]{1,0:T(4,128)S(1)}, s32[4,256]{1,0:T(4,128)}, u32[]{:S(2)}) copy-start(s32[4,256]{1,0:T(4,128)} %get-tuple-element.409) | copy-start | bytes 12292
  62.3 93.9 %copy-start.12 = (s32[4,256]{1,0:T(4,128)S(1)}, s32[4,256]{1,0:T(4,128)}, u32[]{:S(2)}) copy-start(s32[4,256]{1,0:T(4,128)} %get-tuple-element.411) | copy-start | bytes 12292
  62.3 93.9 %copy-start.26 = (s32[4,64]{1,0:T(4,128)S(1)}, s32[4,64]{1,0:T(4,128)}, u32[]{:S(2)}) copy-start(s32[4,64]{1,0:T(4,128)} %add_add_fusion) | copy-start | bytes 3076
  62.3 93.9 %copy-start.28 = (s32[4,64]{1,0:T(4,128)S(1)}, s32[4,64]{1,0:T(4,128)}, u32[]{:S(2)}) copy-start(s32[4,64]{1,0:T(4,128)} %and_select_fusion.1) | copy-start | bytes 3076
  184.4 3.8 copy-start.3
  197.5 3.8 copy-start.3
  210.5 3.8 copy-start.3
  223.6 3.8 copy-start.3
  236.6 3.8 copy-start.3
  262.8 3.8 copy-start.3
  275.8 3.8 copy-start.3
  288.9 3.8 copy-start.3
  301.9 3.8 copy-start.3
  315.0 3.8 copy-start.3
  328.0 3.8 copy-start.3
  341.1 3.8 copy-start.3
  354.1 3.8 copy-start.3
  367.2 3.8 copy-start.3
  380.2 3.8 copy-start.3
  406.4 3.8 copy-start.3
  419.5 3.8 copy-start.3
  432.5 3.8 copy-start.3
  445.6 3.8 copy-start.3
  458.6 3.8 copy-start.3
  471.7 3.8 copy-start.3
  484.7 3.8 copy-start.3
  497.8 3.8 copy-start.3
  510.8 3.8 copy-start.3
  523.9 3.8 copy-start.3
  537.0 3.8 copy-start.3
  550.0 3.8 copy-start.3
  563.1 3.8 copy-start.3
  575.5 189.7 %reduce-scatter.5.cloned.1.call-start = ((), (), s32[]{:S(2)}) async-start(), calls=%async_computation.4 | async-start | bytes 9437184 | tf_op jit(solution)/shard_map/reduce_scatter | solution.py:162
  605.2 12.0 %copy-start.2 = (f32[4,4,64,128]{3,2,1,0:T(8,128)S(1)}, f32[4,4,64,128]{3,2,1,0:T(8,128)}, u32[]{:S(2)}) copy-start(f32[4,4,64,128]{3,2,1,0:T(8,128)} %reduce-scatter.3.cloned.1.call-done) | copy-start | bytes 1572868
  605.2 16.4 %copy-start.17 = (s32[2]{0:T(128)S(1)}, s32[2]{0:T(128)}, u32[]{:S(2)}) copy-start(s32[2]{0:T(128)} %copy-done.16) | copy-start | bytes 28
  606.9 15.0 %copy-start.19 = (s32[2]{0:T(128)S(1)}, s32[2]{0:T(128)}, u32[]{:S(2)}) copy-start(s32[2]{0:T(128)} %copy-done.18) | copy-start | bytes 28
  606.9 22.8 %copy-start.21 = (s32[2]{0:T(128)S(1)}, s32[2]{0:T(128)}, u32[]{:S(2)}) copy-start(s32[2]{0:T(128)} %copy-done.20) | copy-start | bytes 28
  607.0 28.4 %copy-start.23 = (s32[2]{0:T(128)S(1)}, s32[2]{0:T(128)}, u32[]{:S(2)}) copy-start(s32[2]{0:T(128)} %copy-done.22) | copy-start | bytes 28
  607.0 13.4 %collective-permute-start.6 = (f32[2,8192]{1,0:T(2,128)S(1)}, f32[2,8192]{1,0:T(2,128)S(1)}, u32[]{:S(2)}, u32[]{:S(2)}) collective-permute-start(f32[2,8192]{1,0:T(2,128)S(1)} %fusion.39), channel_id=1, source_target_pairs={{4,0},{8,4},{12,8},{16,12},{20,16},{24,20},{28,24},{5,1},{9,5},{13... | collective-permute-start | bytes 196616 | tf_op jit(solution)/shard_map/ppermute | solution.py:17
  609.9 25.8 %copy-start.25 = (s32[2]{0:T(128)S(1)}, s32[2]{0:T(128)}, u32[]{:S(2)}) copy-start(s32[2]{0:T(128)} %copy-done.24) | copy-start | bytes 28
  609.9 26.0 %copy-start.15 = (s32[2]{0:T(128)S(1)}, s32[2]{0:T(128)}, u32[]{:S(2)}) copy-start(s32[2]{0:T(128)} %copy-done.14) | copy-start | bytes 28
  609.9 12.0 %collective-permute-start.8 = (f32[2,8192]{1,0:T(2,128)S(1)}, f32[2,8192]{1,0:T(2,128)S(1)}, u32[]{:S(2)}, u32[]{:S(2)}) collective-permute-start(f32[2,8192]{1,0:T(2,128)S(1)} %fusion.35), channel_id=1, source_target_pairs={{12,0},{16,4},{20,8},{24,12},{28,16},{13,1},{17,5},{21,9},{25,13},... | collective-permute-start | bytes 196616 | tf_op jit(solution)/shard_map/ppermute | solution.py:17
  612.8 17.0 %collective-permute-start.9 = (f32[2,8192]{1,0:T(2,128)S(1)}, f32[2,8192]{1,0:T(2,128)S(1)}, u32[]{:S(2)}, u32[]{:S(2)}) collective-permute-start(f32[2,8192]{1,0:T(2,128)S(1)} %fusion.33), channel_id=1, source_target_pairs={{16,0},{20,4},{24,8},{28,12},{17,1},{21,5},{25,9},{29,13},{18,2},{... | collective-permute-start | bytes 196616 | tf_op jit(solution)/shard_map/ppermute | solution.py:17
  615.9 19.5 %collective-permute-start.10 = (f32[2,8192]{1,0:T(2,128)S(1)}, f32[2,8192]{1,0:T(2,128)S(1)}, u32[]{:S(2)}, u32[]{:S(2)}) collective-permute-start(f32[2,8192]{1,0:T(2,128)S(1)} %fusion.31), channel_id=1, source_target_pairs={{20,0},{24,4},{28,8},{21,1},{25,5},{29,9},{22,2},{26,6},{30,10},{2... | collective-permute-start | bytes 196616 | tf_op jit(solution)/shard_map/ppermute | solution.py:17
  617.8 17.8 %collective-permute-start.11 = (f32[2,8192]{1,0:T(2,128)S(1)}, f32[2,8192]{1,0:T(2,128)S(1)}, u32[]{:S(2)}, u32[]{:S(2)}) collective-permute-start(f32[2,8192]{1,0:T(2,128)S(1)} %fusion.29), channel_id=1, source_target_pairs={{24,0},{28,4},{25,1},{29,5},{26,2},{30,6},{27,3},{31,7}} | collective-permute-start | bytes 196616 | tf_op jit(solution)/shard_map/ppermute | solution.py:17
  620.4 15.6 %collective-permute-start.7 = (f32[2,8192]{1,0:T(2,128)S(1)}, f32[2,8192]{1,0:T(2,128)S(1)}, u32[]{:S(2)}, u32[]{:S(2)}) collective-permute-start(f32[2,8192]{1,0:T(2,128)S(1)} %fusion.37), channel_id=1, source_target_pairs={{8,0},{12,4},{16,8},{20,12},{24,16},{28,20},{9,1},{13,5},{17,9},{2... | collective-permute-start | bytes 196616 | tf_op jit(solution)/shard_map/ppermute | solution.py:17
  (229 other events, 485.7 us)
Sparse Core Ops, SparseCore 0:
  10.2 146.0 all-gather.1
  575.6 29.5 reduce-scatter.2
  609.3 155.8 reduce-scatter.4
where the time goes:
time: 781 us; the launch traced here: 774 us
  matrix products  282 us (36%)
  waiting for transfers between devices  261 us (33%)
  local copies, waits for them, and re-layouts  153 us (20%)
  other arithmetic  33 us (4%)
  starting transfers between devices  25.4 us (3%)
  between operations  14.5 us (2%)
    reduce_scatter x1, waiting for transfers between devices, per_device(): lax.psum_scatter(grad_w_all.astype(jnp.bfloat16), 'fsdp', scatter_dimensi...  128 us
    all_gather x1, waiting for transfers between devices, per_device(): w_piece = lax.all_gather(kv_weight, 'fsdp', axis=1, tiled=True)  90.7 us
    dot_general x32, matrix products, head_pass(): jnp.dot(key_lat, w_head, preferred_element_type=jnp.float32)  57.7 us
    dot_general x32, matrix products, head_pass(): lax.dot_general(grad_kv, w_head, (((1,), (1,)), ((), ())), preferred_elem...  55.5 us
    dot_general x32, matrix products, head_pass(): lax.dot_general(key_lat, grad_kv, (((0,), (0,)), ((), ())), preferred_ele...  53.6 us
    dot_general x32, matrix products, head_pass(): jnp.einsum('qbk,qkd->qbd', probs_low, value_rows, preferred_element_type=...  37.7 us
    dynamic_slice x32, local copies, waits for them, and re-layouts, run_head(): lax.dynamic_index_in_dim(grad_out, head_idx, 1, False)  33.7 us
    dot_general x32, matrix products, head_pass(): jnp.einsum('qbd,qkd->qbk', g_head, value_rows, preferred_element_type=jnp...  28.4 us
  transfers between devices with their start and end apart: 15, of which 6 were waited for; matrix products, arithmetic and copies ran while one was open for 7% of the time, Pallas kernels for 0%

commit v1 on v0

v1 whole, which is shorter than its diff:
```python
import functools

import jax
import jax.numpy as jnp
from jax import lax
from jax.experimental import pallas as pl
from jax.experimental.pallas import tpu as pltpu
from jax.sharding import PartitionSpec as P

BLK = 64
TOPK = 4
DOCS = 4
NEG_FILL = -1e30


def attention_kernel(
    lists_ref, kp_ref, lo_ref, q_ref, g_ref, kv_ref, gq_ref, tok_ref, acc_ref, *, scale
):
    run = pl.program_id(0)
    heads, rows, dk = q_ref.shape
    blocks = rows // BLK

    @pl.when(run == 0)
    def _():
        acc_ref[...] = jnp.zeros_like(acc_ref)

    for b in range(blocks):
        here = slice(b * BLK, (b + 1) * BLK)
        block = run * blocks + b
        idx = [lists_ref[block * TOPK + s] for s in range(TOPK)]
        key_pos = kp_ref[b : b + 1, :]
        pos = block * BLK + lax.broadcasted_iota(jnp.int32, (BLK, TOPK * BLK), 0)
        visible = (key_pos <= pos) & (key_pos >= lo_ref[here, :])
        for h in range(heads):
            q = q_ref[h, here, :]
            g = g_ref[h, here, :]
            zero = jnp.zeros_like(q)
            qg = jnp.concatenate(
                [jnp.concatenate([q, zero], axis=1), jnp.concatenate([zero, g], axis=1)], axis=0
            )
            kv = jnp.concatenate([kv_ref[h, i] for i in idx], axis=0)
            both = lax.dot_general(
                qg, kv, (((1,), (1,)), ((), ())), preferred_element_type=jnp.float32
            )
            scores = jnp.where(visible, both[:BLK] * scale, NEG_FILL)
            top = jnp.max(scores, axis=-1, keepdims=True)
            e = jnp.exp(scores - top)
            probs = e / jnp.sum(e, axis=-1, keepdims=True)
            low = probs.astype(jnp.bfloat16)
            grad_probs = both[BLK:]
            delta = jnp.sum(low.astype(jnp.float32) * grad_probs, axis=-1, keepdims=True)
            ds = (probs * (grad_probs - delta)).astype(jnp.bfloat16)
            gq = jnp.dot(ds, kv[:, :dk], preferred_element_type=jnp.float32)
            gq_ref[h, here, :] = (gq * scale).astype(jnp.bfloat16)
            sides = jnp.concatenate([ds, low], axis=0)
            dkv = lax.dot_general(
                sides, qg, (((0,), (0,)), ((), ())), preferred_element_type=jnp.float32
            )
            for s in range(TOPK):
                acc_ref[h, idx[s]] += dkv[s * BLK : (s + 1) * BLK]

    @pl.when(run == pl.num_programs(0) - 1)
    def _():
        for h in range(heads):
            part = acc_ref[h]
            tok_ref[h, :, :, :dk] = (part[:, :, :dk] * scale).astype(jnp.bfloat16)
            tok_ref[h, :, :, dk:] = part[:, :, dk:].astype(jnp.bfloat16)


def attention(lists, key_pos, lo, q, g, kv):
    runs, heads, rows, dk = q.shape
    nb = kv.shape[1]
    blocks = rows // BLK
    whole = pl.BlockSpec(
        kv.shape, lambda r, lists: (0, 0, 0, 0), pipeline_mode=pl.Buffered(1)
    )
    act = pl.BlockSpec((None, heads, rows, dk), lambda r, lists: (r, 0, 0, 0))
    pairs = nb * heads
    return pl.pallas_call(
        functools.partial(attention_kernel, scale=dk**-0.5),
        grid_spec=pltpu.PrefetchScalarGridSpec(
            num_scalar_prefetch=1,
            grid=(runs,),
            in_specs=[
                pl.BlockSpec((None, blocks, TOPK * BLK), lambda r, lists: (r, 0, 0)),
                pl.BlockSpec((rows, 1), lambda r, lists: (r, 0)),
                act,
                act,
                whole,
            ],
            out_specs=[act, whole],
            scratch_shapes=[pltpu.VMEM(kv.shape, jnp.float32)],
        ),
        out_shape=[
            jax.ShapeDtypeStruct(q.shape, jnp.bfloat16),
            jax.ShapeDtypeStruct(kv.shape, jnp.bfloat16),
        ],
        compiler_params=pltpu.CompilerParams(
            dimension_semantics=("arbitrary",), vmem_limit_bytes=48 * 1024 * 1024
        ),
        cost_estimate=pl.CostEstimate(
            flops=pairs * 5 * 2 * BLK * TOPK * BLK * dk,
            bytes_accessed=3 * 2 * q.size + 4 * kv.size,
            transcendentals=pairs * BLK * TOPK * BLK,
        ),
    )(lists.reshape(-1), key_pos, lo, q, g, kv)


def per_device(latents, queries, grad_out, kv_weight, doc_ids, block_lists):
    n = lax.axis_size("fsdp")
    rows, lat_width = latents.shape
    dk = queries.shape[2]
    heads = kv_weight.shape[1]
    tokens = doc_ids.shape[0]
    nb = tokens // BLK
    w = kv_weight[0]

    all_lat = lax.all_gather(latents, "fsdp", axis=0, tiled=True)

    def by_owner(x):
        return x.reshape(rows, n, heads, dk).transpose(1, 2, 0, 3)

    q = lax.all_to_all(by_owner(queries), "fsdp", 0, 0, tiled=True)
    g = lax.all_to_all(by_owner(grad_out), "fsdp", 0, 0, tiled=True)

    starts = [jnp.sum((doc_ids < v).astype(jnp.int32)) for v in range(DOCS)]
    lo = sum(jnp.where(doc_ids == v, starts[v], 0) for v in range(DOCS))
    key_pos = (block_lists[:, :, None] * BLK + jnp.arange(BLK, dtype=jnp.int32)).reshape(
        n, nb // n, TOPK * BLK
    )

    kv = jnp.einsum("tl,hlk->htk", all_lat, w, preferred_element_type=jnp.float32)
    kv = kv.astype(jnp.bfloat16).reshape(heads, nb, BLK, 2 * dk)
    gq, tok = attention(block_lists, key_pos, lo[:, None], q, g, kv)
    tok = tok.reshape(heads, tokens, 2 * dk)

    lat_part = jnp.einsum("htk,hlk->tl", tok, w, preferred_element_type=jnp.float32)
    shares = lax.psum_scatter(
        lat_part.astype(jnp.bfloat16), "grp", scatter_dimension=1, tiled=True
    )
    grad_latents = lax.psum_scatter(
        shares.astype(jnp.float32), "fsdp", scatter_dimension=0, tiled=True
    )
    back = lax.all_to_all(gq, "fsdp", 0, 0, tiled=True)
    grad_queries = back.transpose(2, 0, 1, 3).reshape(rows, n * heads, dk)
    grad_weight = jnp.einsum("tl,htk->hlk", all_lat, tok, preferred_element_type=jnp.float32)
    return (grad_queries, grad_latents, grad_weight[None])


def solution(mesh):
    return jax.shard_map(
        per_device,
        mesh=mesh,
        in_specs=(
            P("fsdp", None),
            P("fsdp", "grp", None),
            P("fsdp", "grp", None),
            P("grp", "fsdp", None, None),
            P(),
            P(),
        ),
        out_specs=(P("fsdp", "grp", None), P("fsdp", "grp"), P("grp", "fsdp", None, None)),
        check_vma=False,
    )
```

time: 781 us -> 301 us (0.39)
  matrix products: 282 us -> 17 us
  local copies, waits for them, and re-layouts: 153 us -> 26.9 us
  waiting for transfers between devices: 261 us -> 174 us
  Pallas kernels: 0 us -> 47.1 us
  other arithmetic: 33 us -> 5.34 us
  starting transfers between devices: 25.4 us -> 15.9 us
    dot_general x301 -> x3, matrix products: 282 us -> 17 us  [the longest x1 6.54 us: per_device(): jnp.einsum('tl,htk->hlk', all_lat, tok, preferred_element_type=jnp.float32)]
    reduce_scatter x2 -> x1, waiting for transfers between devices: 153 us -> 41 us  [per_device(): lax.psum_scatter(shares.astype(jnp.float32), 'fsdp', scatter_dimension=0,...]
    all_to_all x0 -> x3, waiting for transfers between devices: none -> 105 us  [the longest x1 63 us: per_device(): q = lax.all_to_all(by_owner(queries), 'fsdp', 0, 0, tiled=True)]
    all_gather x1, waiting for transfers between devices: 90.7 us -> 0.02 us  [per_device(): all_lat = lax.all_gather(latents, 'fsdp', axis=0, tiled=True)]
    dynamic_update_slice x96 -> x0, local copies, waits for them, and re-layouts: 48 us -> none  [the longest x64 27.5 us: per_head(): lax.dynamic_update_index_in_dim(grad_w_all, grad_w, head_idx, 0)]
    pallas_call x0 -> x1, Pallas kernels: none -> 47.1 us  [attention(): pl.pallas_call(functools.partial(attention_kernel, scale=dk ** (-0.5)), g...]
    dynamic_slice x33 -> x0, local copies, waits for them, and re-layouts: 34.8 us -> none  [the longest x32 33.7 us: run_head(): lax.dynamic_index_in_dim(grad_out, head_idx, 1, False)]
    unnamed x3 -> x4, waiting for transfers between devices: 1.38 us -> 27.3 us
  transfers between devices with their start and end apart: 15 -> 6, of which waited for: 6 -> 5; matrix products, arithmetic and copies ran while one was open for 7% -> 12% of each run, Pallas kernels for 0% -> 0%
where the time goes in v1:
time: 301 us; the launch traced here: 300 us
  waiting for transfers between devices  174 us (58%)
  Pallas kernels  47.1 us (16%)
  local copies, waits for them, and re-layouts  26.9 us (9%)
  matrix products  17 us (6%)
  starting transfers between devices  15.9 us (5%)
  between operations  13.8 us (5%)
  other arithmetic  5.34 us (2%)
    all_to_all x1, waiting for transfers between devices, per_device(): q = lax.all_to_all(by_owner(queries), 'fsdp', 0, 0, tiled=True)  63 us
    pallas_call x1, Pallas kernels, attention(): pl.pallas_call(functools.partial(attention_kernel, scale=dk ** (-0.5)), g...  47.1 us
    reduce_scatter x1, waiting for transfers between devices, per_device(): lax.psum_scatter(shares.astype(jnp.float32), 'fsdp', scatter_dimension=0,...  41 us
    all_to_all x1, waiting for transfers between devices, per_device(): g = lax.all_to_all(by_owner(grad_out), 'fsdp', 0, 0, tiled=True)  30.3 us
    unnamed x4, waiting for transfers between devices  27.3 us
    unnamed x15, local copies, waits for them, and re-layouts  18.9 us
    all_to_all x1, waiting for transfers between devices, per_device(): back = lax.all_to_all(gq, 'fsdp', 0, 0, tiled=True)  12 us
    all_to_all x1, starting transfers between devices, per_device(): q = lax.all_to_all(by_owner(queries), 'fsdp', 0, 0, tiled=True)  7.28 us
  transfers between devices with their start and end apart: 6, of which 5 were waited for; matrix products, arithmetic and copies ran while one was open for 12% of the time, Pallas kernels for 0%

profile of v1, /device:TPU:0, one launch (start us, length us, event | category | flops | bytes accessed | tf_op | source)
XLA Modules:
  0.0 299.7 jit_solution(4914148843979727128)
XLA Ops:
  7.2 0.0 copy-start
  7.2 3.8 %copy.30 = bf16[256,32,128]{2,0,1:T(8,128)(2,1)} copy(bf16[256,32,128]{2,1,0:T(8,128)(2,1)} %param.7) | data formatting | bytes 4194304 | tf_op args[1]
  11.0 7.3 %all-to-all-start = ((bf16[8,4,256,128]{3,2,1,0:T(8,128)(2,1)}), bf16[8,4,256,128]{3,2,1,0:T(8,128)(2,1)S(1)}, u32[]{:S(2)}, u32[]{:S(2)}) async-start(bf16[8,4,256,128]{3,2,1,0:T(8,128)(2,1)} %bitcast.39), calls=%async_computation | async-start | bytes 4194304 | tf_op jit(solution)/shard_map/all_to_all | solution.py:123
  18.3 0.0 all-gather.2.cloned.1.call-start
  18.3 0.7 all-gather.2.cloned.1.call-update
  19.0 3.7 %copy.31 = bf16[256,32,128]{2,0,1:T(8,128)(2,1)} copy(bf16[256,32,128]{2,1,0:T(8,128)(2,1)} %param.8) | data formatting | bytes 4194304 | tf_op args[2]
  22.7 63.0 %all-to-all-done.q_ref = bf16[8,4,256,128]{3,2,1,0:T(8,128)(2,1)S(1)} async-done(((bf16[8,4,256,128]{3,2,1,0:T(8,128)(2,1)}), bf16[8,4,256,128]{3,2,1,0:T(8,128)(2,1)S(1)}, u32[]{:S(2)}, u32[]{:S(2)}) %all-to-all-start) | async-done | bytes 2097184 | tf_op jit(solution)/shard_map/all_to_all | solution.py:123
  85.7 0.0 copy-start.3
  85.7 0.0 copy-start.2
  85.7 4.5 %all-to-all-start.1 = ((bf16[8,4,256,128]{3,2,1,0:T(8,128)(2,1)}), bf16[8,4,256,128]{3,2,1,0:T(8,128)(2,1)}, u32[]{:S(2)}, u32[]{:S(2)}) async-start(bf16[8,4,256,128]{3,2,1,0:T(8,128)(2,1)} %bitcast.36), calls=%async_computation.1 | async-start | bytes 4194304 | tf_op jit(solution)/shard_map/all_to_all | solution.py:124
  90.2 0.2 reduce-scatter.7.cloned.1.call-start
  90.5 0.1 add.36
  90.6 0.0 copy-done.3
  90.6 0.1 copy.28
  90.6 0.1 copy.29
  90.7 0.1 reshape.29.lists_ref
  90.8 0.1 add.33
  90.9 0.1 add.34
  91.0 0.0 copy-done.2
  91.1 0.7 convert_reduce_fusion.3
  91.8 2.5 select_add_fusion
  94.3 1.3 copy.34.lo_ref
  95.6 0.0 all-gather.2.cloned.1.call-done
  95.7 0.0 copy-done
  95.7 5.9 %convert_bitcast_fusion = bf16[4,2048,256]{1,2,0:T(8,128)(2,1)} fusion(bf16[2048,512]{1,0:T(8,128)(2,1)} %all-gather.2.cloned.1.call-done, bf16[1,4,512,256]{3,2,1,0:T(8,128)(2,1)S(1)} %copy-done), kind=kOutput, calls=%fused_computation.1 | convolution fusion | flops 2149580800 | bytes 7340032 | tf_op jit(solution)/shard_map/tl,hlk->htk/dot_general | solution.py:132
  101.6 6.2 %copy.33 = bf16[4,2048,256]{2,1,0:T(8,128)(2,1)} copy(bf16[4,2048,256]{1,2,0:T(8,128)(2,1)} %convert_bitcast_fusion) | data formatting | bytes 8388608 | tf_op jit(solution)/shard_map/convert_element_type | solution.py:133
  107.8 30.3 %all-to-all-done.1.g_ref = bf16[8,4,256,128]{3,2,1,0:T(8,128)(2,1)} async-done(((bf16[8,4,256,128]{3,2,1,0:T(8,128)(2,1)}), bf16[8,4,256,128]{3,2,1,0:T(8,128)(2,1)}, u32[]{:S(2)}, u32[]{:S(2)}) %all-to-all-start.1) | async-done | bytes 2097184 | tf_op jit(solution)/shard_map/all_to_all | solution.py:124
  138.2 0.0 copy-start.1
  138.2 1.2 copy-done.1
  139.4 47.1 %shard_map.85 = (bf16[8,4,256,128]{3,2,1,0:T(8,128)(2,1)}, bf16[4,32,64,256]{3,2,1,0:T(8,128)(2,1)}) custom-call(s32[128]{0:T(128)S(1)} %reshape.29.lists_ref, s32[8,4,256]{2,1,0:T(4,128)S(1)} %broadcast_add_fusion.kp_ref, s32[2048,1]{1,0:T(8,128)S(1)} %copy-done.1, bf16[8,4,256,128]{3,2,1,0:T(8,128)(2,1)S(1)} %all-to-all-done.q_ref, ...), custom_call_target="tpu_custom_call" | custom-call | flops 2684354560 | bytes 14680064 | tf_op jit(solution)/shard_map/pallas_call | solution.py:79
  186.5 4.6 %bitcast_convert_fusion = bf16[2048,512]{1,0:T(8,128)(2,1)S(1)} fusion(bf16[4,2048,256]{2,1,0:T(8,128)(2,1)} %bitcast.40, bf16[1,4,512,256]{3,2,1,0:T(8,128)(2,1)S(1)} %copy-done), kind=kOutput, calls=%fused_computation | convolution fusion | flops 2148532224 | bytes 7340032 | tf_op jit(solution)/shard_map/htk,hlk->tl/dot_general | solution.py:137
  191.0 2.4 copy.40
  193.4 0.0 reduce-scatter.7.cloned.1.call-update
  193.4 3.6 %all-to-all-start.2 = ((bf16[8,4,256,128]{3,2,1,0:T(8,128)(2,1)}), bf16[8,4,256,128]{3,2,1,0:T(8,128)(2,1)S(1)}, u32[]{:S(2)}, u32[]{:S(2)}) async-start(bf16[8,4,256,128]{3,2,1,0:T(8,128)(2,1)} %get-tuple-element.5), calls=%async_computation.2 | async-start | bytes 4194304 | tf_op jit(solution)/shard_map/all_to_all | solution.py:144
  197.1 0.3 reduce-scatter.5.cloned.1.call-start
  197.3 26.6 %reduce-scatter.7.cloned.1.call-done = bf16[128,2048]{1,0:T(8,128)(2,1)} async-done(((bf16[512,2048]{1,0:T(8,128)(2,1)}), bf16[128,2048]{1,0:T(8,128)(2,1)}) %reduce-scatter.7.cloned.1.call-update) | async-done | bytes 524304
  223.9 2.0 copy.41
  225.9 2.1 convert_element_type.31
  228.0 0.0 reduce-scatter.5.cloned.1.call-update
  228.1 6.5 %fusion.3 = f32[1,4,512,256]{2,3,1,0:T(8,128)} fusion(bf16[4,2048,256]{2,1,0:T(8,128)(2,1)} %bitcast.41, bf16[2048,512]{1,0:T(8,128)(2,1)} %all-gather.2.cloned.1.call-done), kind=kOutput, calls=%fused_computation.5 | convolution fusion | flops 2147483648 | bytes 8388608 | tf_op jit(solution)/shard_map/tl,htk->hlk/dot_general | solution.py:146
  234.6 2.9 copy.37
  237.5 12.0 %all-to-all-done.2 = bf16[8,4,256,128]{3,2,1,0:T(8,128)(2,1)S(1)} async-done(((bf16[8,4,256,128]{3,2,1,0:T(8,128)(2,1)}), bf16[8,4,256,128]{3,2,1,0:T(8,128)(2,1)S(1)}, u32[]{:S(2)}, u32[]{:S(2)}) %all-to-all-start.2) | async-done | bytes 2097184 | tf_op jit(solution)/shard_map/all_to_all | solution.py:144
  249.5 2.7 copy.36
  252.2 41.0 %reduce-scatter.5.cloned.1.call-done = f32[256,128]{1,0:T(8,128)} async-done(((f32[2048,128]{1,0:T(8,128)}), f32[256,128]{1,0:T(8,128)}) %reduce-scatter.5.cloned.1.call-update) | async-done | bytes 131088 | tf_op jit(solution)/shard_map/reduce_scatter | solution.py:141
  (3 shorter events, 0.0 us)
Async XLA Ops:
  7.2 88.5 %copy-start = (bf16[1,4,512,256]{3,2,1,0:T(8,128)(2,1)S(1)}, bf16[1,4,512,256]{3,2,1,0:T(8,128)(2,1)}, u32[]{:S(2)}) copy-start(bf16[1,4,512,256]{3,2,1,0:T(8,128)(2,1)} %param.9) | copy-start | bytes 3145732
  11.0 74.7 %all-to-all-start = ((bf16[8,4,256,128]{3,2,1,0:T(8,128)(2,1)}), bf16[8,4,256,128]{3,2,1,0:T(8,128)(2,1)S(1)}, u32[]{:S(2)}, u32[]{:S(2)}) async-start(bf16[8,4,256,128]{3,2,1,0:T(8,128)(2,1)} %bitcast.39), calls=%async_computation | async-start | bytes 4194304 | tf_op jit(solution)/shard_map/all_to_all | solution.py:123
  18.3 77.4 %all-gather.2.cloned.1.call-start = ((), (), s32[]{:S(2)}) async-start(), calls=%async_computation.5 | async-start | bytes 2359296 | tf_op jit(solution)/shard_map/all_gather | solution.py:118
  85.7 4.8 %copy-start.3 = (s32[32,4]{0,1:T(4,128)S(1)}, s32[32,4]{0,1:T(4,128)}, u32[]{:S(2)}) copy-start(s32[32,4]{0,1:T(4,128)} %param.11) | copy-start | bytes 1540
  85.7 5.3 %copy-start.2 = (s32[2048]{0:T(1024)S(1)}, s32[2048]{0:T(1024)}, u32[]{:S(2)}) copy-start(s32[2048]{0:T(1024)} %param.10) | copy-start | bytes 24580
  85.7 52.4 %all-to-all-start.1 = ((bf16[8,4,256,128]{3,2,1,0:T(8,128)(2,1)}), bf16[8,4,256,128]{3,2,1,0:T(8,128)(2,1)}, u32[]{:S(2)}, u32[]{:S(2)}) async-start(bf16[8,4,256,128]{3,2,1,0:T(8,128)(2,1)} %bitcast.36), calls=%async_computation.1 | async-start | bytes 4194304 | tf_op jit(solution)/shard_map/all_to_all | solution.py:124
  90.2 133.7 %reduce-scatter.7.cloned.1.call-start = ((), (), s32[]{:S(2)}) async-start(), calls=%async_computation.7 | async-start | bytes 2621440
  138.2 1.2 copy-start.1
  193.4 56.1 %all-to-all-start.2 = ((bf16[8,4,256,128]{3,2,1,0:T(8,128)(2,1)}), bf16[8,4,256,128]{3,2,1,0:T(8,128)(2,1)S(1)}, u32[]{:S(2)}, u32[]{:S(2)}) async-start(bf16[8,4,256,128]{3,2,1,0:T(8,128)(2,1)} %get-tuple-element.5), calls=%async_computation.2 | async-start | bytes 4194304 | tf_op jit(solution)/shard_map/all_to_all | solution.py:144
  197.1 96.1 %reduce-scatter.5.cloned.1.call-start = ((), (), s32[]{:S(2)}) async-start(), calls=%async_computation.6 | async-start | bytes 1179648 | tf_op jit(solution)/shard_map/reduce_scatter | solution.py:141
Sparse Core Ops, SparseCore 0:
  21.2 71.0 all-gather.1
  193.5 30.2 reduce-scatter.6
  228.2 64.9 reduce-scatter.4

commit v2 on v1

--- a/solution.py
+++ b/solution.py
@@ -14,10 +14,10 @@
 
 
 def attention_kernel(
-    lists_ref, kp_ref, lo_ref, q_ref, g_ref, kv_ref, gq_ref, tok_ref, acc_ref, *, scale
+    lists_ref, kp_ref, lo_ref, qg_ref, kv_ref, gq_ref, tok_ref, acc_ref, *, scale
 ):
     run = pl.program_id(0)
-    heads, rows, dk = q_ref.shape
+    _, heads, rows, dk = qg_ref.shape
     blocks = rows // BLK
 
     @pl.when(run == 0)
@@ -32,8 +32,8 @@
         pos = block * BLK + lax.broadcasted_iota(jnp.int32, (BLK, TOPK * BLK), 0)
         visible = (key_pos <= pos) & (key_pos >= lo_ref[here, :])
         for h in range(heads):
-            q = q_ref[h, here, :]
-            g = g_ref[h, here, :]
+            q = qg_ref[0, h, here, :]
+            g = qg_ref[1, h, here, :]
             zero = jnp.zeros_like(q)
             qg = jnp.concatenate(
                 [jnp.concatenate([q, zero], axis=1), jnp.concatenate([zero, g], axis=1)], axis=0
@@ -67,8 +67,8 @@
             tok_ref[h, :, :, dk:] = part[:, :, dk:].astype(jnp.bfloat16)
 
 
-def attention(lists, key_pos, lo, q, g, kv):
-    runs, heads, rows, dk = q.shape
+def attention(lists, key_pos, lo, qg, kv):
+    runs, _, heads, rows, dk = qg.shape
     nb = kv.shape[1]
     blocks = rows // BLK
     whole = pl.BlockSpec(
@@ -84,15 +84,14 @@
             in_specs=[
                 pl.BlockSpec((None, blocks, TOPK * BLK), lambda r, lists: (r, 0, 0)),
                 pl.BlockSpec((rows, 1), lambda r, lists: (r, 0)),
-                act,
-                act,
+                pl.BlockSpec((None, 2, heads, rows, dk), lambda r, lists: (r, 0, 0, 0, 0)),
                 whole,
             ],
             out_specs=[act, whole],
             scratch_shapes=[pltpu.VMEM(kv.shape, jnp.float32)],
         ),
         out_shape=[
-            jax.ShapeDtypeStruct(q.shape, jnp.bfloat16),
+            jax.ShapeDtypeStruct((runs, heads, rows, dk), jnp.bfloat16),
             jax.ShapeDtypeStruct(kv.shape, jnp.bfloat16),
         ],
         compiler_params=pltpu.CompilerParams(
@@ -100,10 +99,10 @@
         ),
         cost_estimate=pl.CostEstimate(
             flops=pairs * 5 * 2 * BLK * TOPK * BLK * dk,
-            bytes_accessed=3 * 2 * q.size + 4 * kv.size,
+            bytes_accessed=3 * qg.size + 4 * kv.size,
             transcendentals=pairs * BLK * TOPK * BLK,
         ),
-    )(lists.reshape(-1), key_pos, lo, q, g, kv)
+    )(lists.reshape(-1), key_pos, lo, qg, kv)
 
 
 def per_device(latents, queries, grad_out, kv_weight, doc_ids, block_lists):
@@ -113,15 +112,25 @@
     heads = kv_weight.shape[1]
     tokens = doc_ids.shape[0]
     nb = tokens // BLK
-    w = kv_weight[0]
 
     all_lat = lax.all_gather(latents, "fsdp", axis=0, tiled=True)
 
-    def by_owner(x):
-        return x.reshape(rows, n, heads, dk).transpose(1, 2, 0, 3)
+    sizes = [h for h in (heads // 2, heads - heads // 2) if h]
+    spans = [slice(sum(sizes[:i]), sum(sizes[: i + 1])) for i in range(len(sizes))]
 
-    q = lax.all_to_all(by_owner(queries), "fsdp", 0, 0, tiled=True)
-    g = lax.all_to_all(by_owner(grad_out), "fsdp", 0, 0, tiled=True)
+    def by_owner(x, span):
+        return x.reshape(rows, n, heads, dk)[:, :, span].transpose(1, 2, 0, 3)
+
+    arrived = [
+        lax.all_to_all(
+            jnp.stack([by_owner(queries, span), by_owner(grad_out, span)], axis=1),
+            "fsdp",
+            0,
+            0,
+            tiled=True,
+        )
+        for span in spans
+    ]
 
     starts = [jnp.sum((doc_ids < v).astype(jnp.int32)) for v in range(DOCS)]
     lo = sum(jnp.where(doc_ids == v, starts[v], 0) for v in range(DOCS))
@@ -129,21 +138,27 @@
         n, nb // n, TOPK * BLK
     )
 
-    kv = jnp.einsum("tl,hlk->htk", all_lat, w, preferred_element_type=jnp.float32)
-    kv = kv.astype(jnp.bfloat16).reshape(heads, nb, BLK, 2 * dk)
-    gq, tok = attention(block_lists, key_pos, lo[:, None], q, g, kv)
-    tok = tok.reshape(heads, tokens, 2 * dk)
+    back, grad_w, lat_part = [], [], 0.0
+    for span, qg in zip(spans, arrived):
+        w = kv_weight[0, span]
+        kv = jnp.einsum("tl,hlk->htk", all_lat, w, preferred_element_type=jnp.float32)
+        kv = kv.astype(jnp.bfloat16).reshape(-1, nb, BLK, 2 * dk)
+        gq, tok = attention(block_lists, key_pos, lo[:, None], qg, kv)
+        back.append(lax.all_to_all(gq, "fsdp", 0, 0, tiled=True))
+        tok = tok.reshape(-1, tokens, 2 * dk)
+        lat_part += jnp.einsum("htk,hlk->tl", tok, w, preferred_element_type=jnp.float32)
+        grad_w.append(
+            jnp.einsum("tl,htk->hlk", all_lat, tok, preferred_element_type=jnp.float32)
+        )
 
-    lat_part = jnp.einsum("htk,hlk->tl", tok, w, preferred_element_type=jnp.float32)
     shares = lax.psum_scatter(
         lat_part.astype(jnp.bfloat16), "grp", scatter_dimension=1, tiled=True
     )
-    grad_latents = lax.psum_scatter(
-        shares.astype(jnp.float32), "fsdp", scatter_dimension=0, tiled=True
-    )
-    back = lax.all_to_all(gq, "fsdp", 0, 0, tiled=True)
-    grad_queries = back.transpose(2, 0, 1, 3).reshape(rows, n * heads, dk)
-    grad_weight = jnp.einsum("tl,htk->hlk", all_lat, tok, preferred_element_type=jnp.float32)
+    pieces = lax.all_to_all(shares.reshape(n, rows, -1), "fsdp", 0, 0, tiled=True)
+    grad_latents = jnp.sum(pieces.astype(jnp.float32), axis=0)
+    grad_queries = jnp.concatenate([x.transpose(2, 0, 1, 3) for x in back], axis=2)
+    grad_queries = grad_queries.reshape(rows, n * heads, dk)
+    grad_weight = jnp.concatenate(grad_w, axis=0)
     return (grad_queries, grad_latents, grad_weight[None])
 
 

time: 301 us -> 264 us (0.88)
  waiting for transfers between devices: 174 us -> 90.9 us
  blocking collectives: 0 us -> 30.5 us
  other arithmetic: 5.34 us -> 9.46 us
  starting transfers between devices: 15.9 us -> 19.8 us
  local copies, waits for them, and re-layouts: 26.9 us -> 30.6 us
    reduce_scatter x1 -> x0, waiting for transfers between devices: 41 us -> none  [per_device(): lax.psum_scatter(shares.astype(jnp.float32), 'fsdp', scatter_dimension=0,...]
    all_to_all x0 -> x1, blocking collectives: none -> 30.5 us  [per_device(): back.append(lax.all_to_all(gq, 'fsdp', 0, 0, tiled=True))]
    unnamed x4 -> x3, waiting for transfers between devices: 27.3 us -> 0.72 us
    all_to_all x3 -> x4, waiting for transfers between devices: 105 us -> 90.2 us  [the longest x2 64 us: per_device(): lax.all_to_all(jnp.stack([by_owner(queries, span), by_owner(grad_out, spa...]
    all_to_all x3 -> x4, starting transfers between devices: 15.4 us -> 19.5 us  [the longest x2 11.6 us: per_device(): lax.all_to_all(jnp.stack([by_owner(queries, span), by_owner(grad_out, spa...]
    dot_general x1 -> x2, matrix products: 5.93 us -> 8.07 us  [per_device(): jnp.einsum('tl,hlk->htk', all_lat, w, preferred_element_type=jnp.float32)]
    pallas_call x1 -> x2, Pallas kernels: 47.1 us -> 49.1 us  [attention(): pl.pallas_call(functools.partial(attention_kernel, scale=dk ** (-0.5)), g...]
    convert_element_type x1 -> x2, local copies, waits for them, and re-layouts: 6.22 us -> 8.06 us  [per_device(): kv = kv.astype(jnp.bfloat16).reshape(-1, nb, BLK, 2 * dk)]
  transfers between devices with their start and end apart: 6 -> 6, of which waited for: 5 -> 3; matrix products, arithmetic and copies ran while one was open for 12% -> 15% of each run, Pallas kernels for 0% -> 9%
where the time goes in v2:
time: 264 us; the launch traced here: 263 us
  waiting for transfers between devices  90.9 us (34%)
  Pallas kernels  49.1 us (19%)
  local copies, waits for them, and re-layouts  30.6 us (12%)
  blocking collectives  30.5 us (12%)
  starting transfers between devices  19.8 us (8%)
  matrix products  18.8 us (7%)
  between operations  14.2 us (5%)
  other arithmetic  9.46 us (4%)
    all_to_all x2, waiting for transfers between devices, per_device(): lax.all_to_all(jnp.stack([by_owner(queries, span), by_owner(grad_out, spa...  64 us
    pallas_call x2, Pallas kernels, attention(): pl.pallas_call(functools.partial(attention_kernel, scale=dk ** (-0.5)), g...  49.1 us
    all_to_all x1, blocking collectives, per_device(): back.append(lax.all_to_all(gq, 'fsdp', 0, 0, tiled=True))  30.5 us
    all_to_all x1, waiting for transfers between devices, per_device(): back.append(lax.all_to_all(gq, 'fsdp', 0, 0, tiled=True))  23.4 us
    unnamed x35, local copies, waits for them, and re-layouts  18.9 us
    all_to_all x2, starting transfers between devices, per_device(): lax.all_to_all(jnp.stack([by_owner(queries, span), by_owner(grad_out, spa...  11.6 us
    dot_general x2, matrix products, per_device(): jnp.einsum('tl,hlk->htk', all_lat, w, preferred_element_type=jnp.float32)  8.07 us
    convert_element_type x2, local copies, waits for them, and re-layouts, per_device(): kv = kv.astype(jnp.bfloat16).reshape(-1, nb, BLK, 2 * dk)  8.06 us
  transfers between devices with their start and end apart: 6, of which 3 were waited for; matrix products, arithmetic and copies ran while one was open for 15% of the time, Pallas kernels for 9%

profile of v2, /device:TPU:0, one launch (start us, length us, event | category | flops | bytes accessed | tf_op | source)
XLA Modules:
  0.0 263.4 jit_solution(2738543798704661731)
XLA Ops:
  7.2 0.0 copy-start.9
  7.2 2.6 copy.46
  9.7 0.0 copy-done.9
  9.7 0.8 copy.45
  10.6 1.4 slice_bitcast_fusion.2
  12.0 0.2 pad_maximum_fusion
  12.2 1.5 copy.47
  13.6 7.3 %all-to-all-start = ((bf16[8,2,2,256,128]{4,3,2,1,0:T(8,128)(2,1)}), bf16[8,2,2,256,128]{4,3,2,1,0:T(8,128)(2,1)S(1)}, u32[]{:S(2)}, u32[]{:S(2)}) async-start(bf16[8,2,2,256,128]{4,3,2,1,0:T(8,128)(2,1)} %copy.47), calls=%async_computation | async-start | bytes 4194304 | tf_op jit(solution)/shard_map/all_to_all | solution.py:125
  20.9 0.0 all-gather.2.cloned.1.call-start
  21.0 0.7 all-gather.2.cloned.1.call-update
  21.7 2.7 %pad_maximum_fusion.1 = bf16[8,2,2,256,128]{4,3,2,1,0:T(8,128)(2,1)} fusion(bf16[8,1,2,256,128]{4,3,2,1,0:T(8,128)(2,1)S(1)} %get-tuple-element.27, bf16[8,1,2,256,128]{4,3,2,1,0:T(8,128)(2,1)} %get-tuple-element.28), kind=kLoop, calls=%fused_computation.7 | loop fusion | flops 1048576 | bytes 4194304 | tf_op jit(solution)/shard_map/stack | solution.py:126
  24.4 64.0 %all-to-all-done.qg_ref = bf16[8,2,2,256,128]{4,3,2,1,0:T(8,128)(2,1)S(1)} async-done(((bf16[8,2,2,256,128]{4,3,2,1,0:T(8,128)(2,1)}), bf16[8,2,2,256,128]{4,3,2,1,0:T(8,128)(2,1)S(1)}, u32[]{:S(2)}, u32[]{:S(2)}) %all-to-all-start) | async-done | bytes 2097184 | tf_op jit(solution)/shard_map/all_to_all | solution.py:125
  88.4 1.3 copy-done.6
  89.7 4.3 %all-to-all-start.2 = ((bf16[8,2,2,256,128]{4,3,2,1,0:T(8,128)(2,1)}), bf16[8,2,2,256,128]{4,3,2,1,0:T(8,128)(2,1)}, u32[]{:S(2)}, u32[]{:S(2)}) async-start(bf16[8,2,2,256,128]{4,3,2,1,0:T(8,128)(2,1)} %pad_maximum_fusion.1), calls=%async_computation.2 | async-start | bytes 4194304 | tf_op jit(solution)/shard_map/all_to_all | solution.py:125
  94.1 0.2 reduce-scatter.4.cloned.1.call-start
  94.3 0.0 copy-done.13
  94.3 0.1 copy.43
  94.4 0.1 reshape.41.lists_ref
  94.5 0.1 copy.44
  94.6 0.1 add.34
  94.7 0.1 add.35
  94.8 0.1 add.37
  94.9 0.0 copy-done.12
  94.9 0.7 convert_reduce_fusion.4
  95.6 2.5 select_add_fusion
  98.1 0.4 copy.50.lo_ref
  98.5 0.0 all-gather.2.cloned.1.call-done
  98.5 4.4 %fusion.2 = bf16[2,2048,256]{1,2,0:T(8,128)(2,1)} fusion(bf16[2048,512]{1,0:T(8,128)(2,1)} %all-gather.2.cloned.1.call-done, bf16[1,4,512,256]{3,2,1,0:T(8,128)(2,1)} %param.9), kind=kOutput, calls=%fused_computation.5 | convolution fusion | flops 1074790400 | bytes 4718592 | tf_op jit(solution)/shard_map/tl,hlk->htk/dot_general | solution.py:144
  102.9 4.1 %copy.53 = bf16[2,2048,256]{2,1,0:T(8,128)(2,1)} copy(bf16[2,2048,256]{1,2,0:T(8,128)(2,1)} %fusion.2) | data formatting | bytes 4194304 | tf_op jit(solution)/shard_map/convert_element_type | solution.py:145
  107.0 0.0 copy-done.4
  107.0 3.7 %fusion.1 = bf16[2,2048,256]{1,2,0:T(8,128)(2,1)} fusion(bf16[2048,512]{1,0:T(8,128)(2,1)S(1)} %copy-done.4, bf16[1,4,512,256]{3,2,1,0:T(8,128)(2,1)} %param.9), kind=kOutput, calls=%fused_computation.4 | convolution fusion | flops 1074790400 | bytes 4718592 | tf_op jit(solution)/shard_map/tl,hlk->htk/dot_general | solution.py:144
  110.7 4.0 %copy.49 = bf16[2,2048,256]{2,1,0:T(8,128)(2,1)} copy(bf16[2,2048,256]{1,2,0:T(8,128)(2,1)} %fusion.1) | data formatting | bytes 4194304 | tf_op jit(solution)/shard_map/convert_element_type | solution.py:145
  114.6 24.7 %shard_map.85 = (bf16[8,2,256,128]{3,2,1,0:T(8,128)(2,1)}, bf16[2,32,64,256]{3,2,1,0:T(8,128)(2,1)S(1)}) custom-call(s32[128]{0:T(128)S(1)} %reshape.41.lists_ref, s32[8,4,256]{2,1,0:T(4,128)S(1)} %broadcast_add_fusion.kp_ref, s32[2048,1]{1,0:T(8,128)S(1)} %copy.50.lo_ref, bf16[8,2,2,256,128]{4,3,2,1,0:T(8,128)(2,1)} %copy-done.6, ...), custom_call_target="tpu_custom_call" | custom-call | flops 1342177280 | bytes 7340032 | tf_op jit(solution)/shard_map/pallas_call | solution.py:79
  139.4 0.0 copy-done.10
  139.4 3.2 %fusion.17 = f32[2048,512,1]{1,0,2:T(8,128)} fusion(bf16[2,2048,256]{2,1,0:T(8,128)(2,1)S(1)} %bitcast.78, bf16[1,4,512,256]{3,2,1,0:T(8,128)(2,1)S(1)} %copy-done.10), kind=kOutput, calls=%fused_computation.25 | convolution fusion | flops 1073741824 | bytes 6815744 | tf_op jit(solution)/shard_map/htk,hlk->tl/dot_general | solution.py:149
  142.6 0.0 all-to-all-done.2.qg_ref
  142.6 24.3 %shard_map.86 = (bf16[8,2,256,128]{3,2,1,0:T(8,128)(2,1)S(1)}, bf16[2,32,64,256]{3,2,1,0:T(8,128)(2,1)S(1)}) custom-call(s32[128]{0:T(128)S(1)} %reshape.41.lists_ref, s32[8,4,256]{2,1,0:T(4,128)S(1)} %broadcast_add_fusion.kp_ref, s32[2048,1]{1,0:T(8,128)S(1)} %copy.50.lo_ref, bf16[8,2,2,256,128]{4,3,2,1,0:T(8,128)(2,1)} %all-to-all-done.2.qg_ref, ...), custom_call_target="tpu_custom_call" | custom-call | flops 1342177280 | bytes 7340032 | tf_op jit(solution)/shard_map/pallas_call | solution.py:79
  166.9 0.0 copy-start.1
  166.9 1.1 copy-done.1
  168.0 1.3 copy-done
  169.3 0.0 copy-done.3
  169.3 0.0 copy-done.11
  169.3 2.6 fusion
  172.0 3.9 %copy.65 = bf16[2048,512]{0,1:T(8,128)(2,1)} copy(bf16[2048,512]{1,0:T(8,128)(2,1)} %fusion) | data formatting | bytes 4194304
  175.9 0.0 reduce-scatter.4.cloned.1.call-update
  175.9 1.2 copy-done.2
  177.1 30.5 %all_to_all.25 = bf16[8,2,256,128]{3,2,1,0:T(8,128)(2,1)} all-to-all(bf16[8,2,256,128]{3,2,1,0:T(8,128)(2,1)S(1)} %copy-done.2), channel_id=1, replica_groups=mesh['fsdp'=8,'grp'=4] {'fsdp'}, dimensions={0} | all-to-all | bytes 2097152 | tf_op jit(solution)/shard_map/all_to_all | solution.py:147
  207.6 3.6 %all-to-all-start.1 = ((bf16[8,2,256,128]{3,2,1,0:T(8,128)(2,1)}), bf16[8,2,256,128]{3,2,1,0:T(8,128)(2,1)S(1)}, u32[]{:S(2)}, u32[]{:S(2)}) async-start(bf16[8,2,256,128]{3,2,1,0:T(8,128)(2,1)} %get-tuple-element.7), calls=%async_computation.1 | async-start | bytes 2097152 | tf_op jit(solution)/shard_map/all_to_all | solution.py:147
  211.1 0.0 reduce-scatter.4.cloned.1.call-done
  211.2 2.0 copy.66
  213.2 23.4 %all-to-all-done.1 = bf16[8,2,256,128]{3,2,1,0:T(8,128)(2,1)S(1)} async-done(((bf16[8,2,256,128]{3,2,1,0:T(8,128)(2,1)}), bf16[8,2,256,128]{3,2,1,0:T(8,128)(2,1)S(1)}, u32[]{:S(2)}, u32[]{:S(2)}) %all-to-all-start.1) | async-done | bytes 1048608 | tf_op jit(solution)/shard_map/all_to_all | solution.py:147
  236.6 4.4 %all-to-all-start.4 = ((bf16[8,256,128]{2,1,0:T(8,128)(2,1)}), bf16[8,256,128]{2,1,0:T(8,128)(2,1)}, u32[]{:S(2)}, u32[]{:S(2)}) async-start(bf16[8,256,128]{2,1,0:T(8,128)(2,1)} %bitcast.90), calls=%async_computation.4 | async-start | bytes 1048576 | tf_op jit(solution)/shard_map/all_to_all | solution.py:157
  241.0 0.0 copy-start.5
  241.0 3.6 %fusion.12 = f32[2,512,256]{1,2,0:T(8,128)S(1)} fusion(bf16[2,2048,256]{2,1,0:T(8,128)(2,1)} %bitcast.81, bf16[2048,512]{1,0:T(8,128)(2,1)} %all-gather.2.cloned.1.call-done), kind=kOutput, calls=%fused_computation.17 | convolution fusion | flops 1073741824 | bytes 5242880 | tf_op jit(solution)/shard_map/tl,htk->hlk/dot_general | solution.py:151
  244.7 0.0 copy-done.8
  244.7 0.0 copy-done.5
  244.7 1.3 fusion.9
  245.9 0.2 maximum_bitcast_fusion
  246.1 0.0 copy-start.7
  246.1 1.8 copy.60
  248.0 1.4 pad_maximum_fusion.2
  249.4 2.7 %copy.59 = bf16[256,32,128]{2,1,0:T(8,128)(2,1)} copy(bf16[256,32,128]{2,0,1:T(8,128)(2,1)S(1)} %bitcast.85) | data formatting | bytes 4194304
  252.0 2.8 %all-to-all-done.4 = bf16[8,256,128]{2,1,0:T(8,128)(2,1)} async-done(((bf16[8,256,128]{2,1,0:T(8,128)(2,1)}), bf16[8,256,128]{2,1,0:T(8,128)(2,1)}, u32[]{:S(2)}, u32[]{:S(2)}) %all-to-all-start.4) | async-done | bytes 524320 | tf_op jit(solution)/shard_map/all_to_all | solution.py:157
  254.8 1.8 convert_reduce_fusion
  (14 shorter events, 0.0 us)
Async XLA Ops:
  7.2 2.6 copy-start.9
  13.6 74.7 %all-to-all-start = ((bf16[8,2,2,256,128]{4,3,2,1,0:T(8,128)(2,1)}), bf16[8,2,2,256,128]{4,3,2,1,0:T(8,128)(2,1)S(1)}, u32[]{:S(2)}, u32[]{:S(2)}) async-start(bf16[8,2,2,256,128]{4,3,2,1,0:T(8,128)(2,1)} %copy.47), calls=%async_computation | async-start | bytes 4194304 | tf_op jit(solution)/shard_map/all_to_all | solution.py:125
  20.9 77.6 %all-gather.2.cloned.1.call-start = ((), (), s32[]{:S(2)}) async-start(), calls=%async_computation.6 | async-start | bytes 2359296 | tf_op jit(solution)/shard_map/all_gather | solution.py:116
  24.4 69.9 %copy-start.13 = (s32[32,4]{0,1:T(4,128)S(1)}, s32[32,4]{0,1:T(4,128)}, u32[]{:S(2)}) copy-start(s32[32,4]{0,1:T(4,128)} %param.11) | copy-start | bytes 1540
  24.4 70.5 %copy-start.12 = (s32[2048]{0:T(1024)S(1)}, s32[2048]{0:T(1024)}, u32[]{:S(2)}) copy-start(s32[2048]{0:T(1024)} %param.10) | copy-start | bytes 24580
  88.4 1.3 copy-start.6
  89.7 52.9 %all-to-all-start.2 = ((bf16[8,2,2,256,128]{4,3,2,1,0:T(8,128)(2,1)}), bf16[8,2,2,256,128]{4,3,2,1,0:T(8,128)(2,1)}, u32[]{:S(2)}, u32[]{:S(2)}) async-start(bf16[8,2,2,256,128]{4,3,2,1,0:T(8,128)(2,1)} %pad_maximum_fusion.1), calls=%async_computation.2 | async-start | bytes 4194304 | tf_op jit(solution)/shard_map/all_to_all | solution.py:125
  94.1 117.1 %reduce-scatter.4.cloned.1.call-start = ((), (), s32[]{:S(2)}) async-start(), calls=%async_computation.7 | async-start | bytes 2621440
  102.9 4.1 %copy-start.4 = (bf16[2048,512]{1,0:T(8,128)(2,1)S(1)}, bf16[2048,512]{1,0:T(8,128)(2,1)}, u32[]{:S(2)}) copy-start(bf16[2048,512]{1,0:T(8,128)(2,1)} %all-gather.2.cloned.1.call-done) | copy-start | bytes 6291460
  114.6 24.8 %copy-start.10 = (bf16[1,4,512,256]{3,2,1,0:T(8,128)(2,1)S(1)}, bf16[1,4,512,256]{3,2,1,0:T(8,128)(2,1)}, u32[]{:S(2)}) copy-start(bf16[1,4,512,256]{3,2,1,0:T(8,128)(2,1)} %param.9) | copy-start | bytes 3145732
  142.6 26.7 %copy-start.3 = (f32[2048,512,1]{1,0,2:T(8,128)S(1)}, f32[2048,512,1]{1,0,2:T(8,128)}, u32[]{:S(2)}) copy-start(f32[2048,512,1]{1,0,2:T(8,128)} %fusion.17) | copy-start | bytes 12582916
  142.6 26.7 %copy-start.11 = (bf16[1,4,512,256]{3,2,1,0:T(8,128)(2,1)S(1)}, bf16[1,4,512,256]{3,2,1,0:T(8,128)(2,1)}, u32[]{:S(2)}) copy-start(bf16[1,4,512,256]{3,2,1,0:T(8,128)(2,1)} %param.9) | copy-start | bytes 3145732
  166.9 1.1 copy-start.1
  168.0 1.3 copy-start
  175.9 1.2 copy-start.2
  207.6 29.0 %all-to-all-start.1 = ((bf16[8,2,256,128]{3,2,1,0:T(8,128)(2,1)}), bf16[8,2,256,128]{3,2,1,0:T(8,128)(2,1)S(1)}, u32[]{:S(2)}, u32[]{:S(2)}) async-start(bf16[8,2,256,128]{3,2,1,0:T(8,128)(2,1)} %get-tuple-element.7), calls=%async_computation.1 | async-start | bytes 2097152 | tf_op jit(solution)/shard_map/all_to_all | solution.py:147
  236.6 8.0 %copy-start.8 = (bf16[8,2,256,128]{3,2,1,0:T(8,128)(2,1)}, bf16[8,2,256,128]{3,2,1,0:T(8,128)(2,1)S(1)}, u32[]{:S(2)}) copy-start(bf16[8,2,256,128]{3,2,1,0:T(8,128)(2,1)S(1)} %all-to-all-done.1) | copy-start | bytes 3145732
  236.6 18.2 %all-to-all-start.4 = ((bf16[8,256,128]{2,1,0:T(8,128)(2,1)}), bf16[8,256,128]{2,1,0:T(8,128)(2,1)}, u32[]{:S(2)}, u32[]{:S(2)}) async-start(bf16[8,256,128]{2,1,0:T(8,128)(2,1)} %bitcast.90), calls=%async_computation.4 | async-start | bytes 1048576 | tf_op jit(solution)/shard_map/all_to_all | solution.py:157
  241.0 3.7 %copy-start.5 = (bf16[2048,512]{1,0:T(8,128)(2,1)S(1)}, bf16[2048,512]{1,0:T(8,128)(2,1)}, u32[]{:S(2)}) copy-start(bf16[2048,512]{1,0:T(8,128)(2,1)} %all-gather.2.cloned.1.call-done) | copy-start | bytes 6291460
  246.1 1.8 copy-start.7
Sparse Core Ops, SparseCore 0:
  23.9 71.0 all-gather.1
  176.0 32.5 reduce-scatter.3

commit v3 on v2

--- a/solution.py
+++ b/solution.py
@@ -146,14 +146,13 @@
         gq, tok = attention(block_lists, key_pos, lo[:, None], qg, kv)
         back.append(lax.all_to_all(gq, "fsdp", 0, 0, tiled=True))
         tok = tok.reshape(-1, tokens, 2 * dk)
-        lat_part += jnp.einsum("htk,hlk->tl", tok, w, preferred_element_type=jnp.float32)
+        lat_part += jnp.einsum("hlk,htk->lt", w, tok, preferred_element_type=jnp.float32)
         grad_w.append(
             jnp.einsum("tl,htk->hlk", all_lat, tok, preferred_element_type=jnp.float32)
         )
 
-    shares = lax.psum_scatter(
-        lat_part.astype(jnp.bfloat16), "grp", scatter_dimension=1, tiled=True
-    )
+    lat_low, back[0] = lax.optimization_barrier((lat_part.astype(jnp.bfloat16), back[0]))
+    shares = lax.psum_scatter(lat_low, "grp", scatter_dimension=0, tiled=True).T
     pieces = lax.all_to_all(shares.reshape(n, rows, -1), "fsdp", 0, 0, tiled=True)
     grad_latents = jnp.sum(pieces.astype(jnp.float32), axis=0)
     grad_queries = jnp.concatenate([x.transpose(2, 0, 1, 3) for x in back], axis=2)

time: 264 us -> 252 us (0.955)
  blocking collectives: 30.5 us -> 0 us
  waiting for transfers between devices: 90.9 us -> 108 us
  starting transfers between devices: 19.8 us -> 27.3 us
  local copies, waits for them, and re-layouts: 30.6 us -> 26.5 us
    all_to_all x1 -> x0, blocking collectives: 30.5 us -> none  [per_device(): back.append(lax.all_to_all(gq, 'fsdp', 0, 0, tiled=True))]
    unnamed x3, waiting for transfers between devices: 0.72 us -> 27.5 us
    all_to_all x1 -> x2, waiting for transfers between devices: 23.4 us -> 0.01 us  [per_device(): back.append(lax.all_to_all(gq, 'fsdp', 0, 0, tiled=True))]
    all_to_all x2, waiting for transfers between devices: 64 us -> 76.9 us  [per_device(): lax.all_to_all(jnp.stack([by_owner(queries, span), by_owner(grad_out, spa...]
    all_to_all x1 -> x2, starting transfers between devices: 3.56 us -> 9.92 us  [per_device(): back.append(lax.all_to_all(gq, 'fsdp', 0, 0, tiled=True))]
    unnamed x35 -> x23, local copies, waits for them, and re-layouts: 18.9 us -> 16.3 us
  transfers between devices with their start and end apart: 6 -> 7, of which waited for: 3 -> 4; matrix products, arithmetic and copies ran while one was open for 15% -> 15% of each run, Pallas kernels for 9% -> 19%
where the time goes in v3:
time: 252 us; the launch traced here: 251 us
  waiting for transfers between devices  108 us (43%)
  Pallas kernels  48.8 us (19%)
  starting transfers between devices  27.3 us (11%)
  local copies, waits for them, and re-layouts  26.5 us (11%)
  matrix products  16.3 us (6%)
  between operations  14.2 us (6%)
  other arithmetic  9.65 us (4%)
    all_to_all x2, waiting for transfers between devices, per_device(): lax.all_to_all(jnp.stack([by_owner(queries, span), by_owner(grad_out, spa...  76.9 us
    pallas_call x2, Pallas kernels, attention(): pl.pallas_call(functools.partial(attention_kernel, scale=dk ** (-0.5)), g...  48.8 us
    unnamed x3, waiting for transfers between devices  27.5 us
    unnamed x23, local copies, waits for them, and re-layouts  16.3 us
    all_to_all x2, starting transfers between devices, per_device(): lax.all_to_all(jnp.stack([by_owner(queries, span), by_owner(grad_out, spa...  11.6 us
    all_to_all x2, starting transfers between devices, per_device(): back.append(lax.all_to_all(gq, 'fsdp', 0, 0, tiled=True))  9.92 us
    dot_general x2, matrix products, per_device(): jnp.einsum('tl,hlk->htk', all_lat, w, preferred_element_type=jnp.float32)  7.47 us
    convert_element_type x2, local copies, waits for them, and re-layouts, per_device(): kv = kv.astype(jnp.bfloat16).reshape(-1, nb, BLK, 2 * dk)  6.48 us
  transfers between devices with their start and end apart: 7, of which 4 were waited for; matrix products, arithmetic and copies ran while one was open for 15% of the time, Pallas kernels for 19%

profile of v3, /device:TPU:0, one launch (start us, length us, event | category | flops | bytes accessed | tf_op | source)
XLA Modules:
  0.0 250.7 jit_solution(1058942573090575883)
XLA Ops:
  7.2 0.0 copy-start.4
  7.2 2.6 %copy.46 = bf16[256,32,128]{2,0,1:T(8,128)(2,1)S(1)} copy(bf16[256,32,128]{2,1,0:T(8,128)(2,1)} %param.8) | data formatting | bytes 4194304 | tf_op args[2]
  9.7 0.0 copy-done.4
  9.7 0.8 copy.45
  10.6 1.4 slice_bitcast_fusion.2
  12.0 0.2 pad_maximum_fusion
  12.2 1.5 copy.47
  13.6 7.3 %all-to-all-start = ((bf16[8,2,2,256,128]{4,3,2,1,0:T(8,128)(2,1)}), bf16[8,2,2,256,128]{4,3,2,1,0:T(8,128)(2,1)S(1)}, u32[]{:S(2)}, u32[]{:S(2)}) async-start(bf16[8,2,2,256,128]{4,3,2,1,0:T(8,128)(2,1)} %copy.47), calls=%async_computation | async-start | bytes 4194304 | tf_op jit(solution)/shard_map/all_to_all | solution.py:125
  20.9 0.0 all-gather.2.cloned.1.call-start
  21.0 0.7 all-gather.2.cloned.1.call-update
  21.7 2.7 %pad_maximum_fusion.1 = bf16[8,2,2,256,128]{4,3,2,1,0:T(8,128)(2,1)} fusion(bf16[8,1,2,256,128]{4,3,2,1,0:T(8,128)(2,1)S(1)} %get-tuple-element.31, bf16[8,1,2,256,128]{4,3,2,1,0:T(8,128)(2,1)} %get-tuple-element.32), kind=kLoop, calls=%fused_computation.8 | loop fusion | flops 1048576 | bytes 4194304 | tf_op jit(solution)/shard_map/stack | solution.py:126
  24.4 0.0 copy-start.7
  24.4 0.0 copy-start.6
  24.4 64.0 %all-to-all-done.qg_ref = bf16[8,2,2,256,128]{4,3,2,1,0:T(8,128)(2,1)S(1)} async-done(((bf16[8,2,2,256,128]{4,3,2,1,0:T(8,128)(2,1)}), bf16[8,2,2,256,128]{4,3,2,1,0:T(8,128)(2,1)S(1)}, u32[]{:S(2)}, u32[]{:S(2)}) %all-to-all-start) | async-done | bytes 2097184 | tf_op jit(solution)/shard_map/all_to_all | solution.py:125
  88.4 0.0 copy-start.3
  88.4 1.3 copy-done.3
  89.7 4.3 %all-to-all-start.1 = ((bf16[8,2,2,256,128]{4,3,2,1,0:T(8,128)(2,1)}), bf16[8,2,2,256,128]{4,3,2,1,0:T(8,128)(2,1)}, u32[]{:S(2)}, u32[]{:S(2)}) async-start(bf16[8,2,2,256,128]{4,3,2,1,0:T(8,128)(2,1)} %pad_maximum_fusion.1), calls=%async_computation.1 | async-start | bytes 4194304 | tf_op jit(solution)/shard_map/all_to_all | solution.py:125
  94.1 0.0 copy-done.7
  94.1 0.1 copy.43
  94.2 0.1 reshape.41.lists_ref
  94.3 0.1 copy.44
  94.4 0.1 add.35
  94.5 0.1 add.36
  94.6 0.1 add.38
  94.7 0.0 copy-done.6
  94.7 0.8 convert_reduce_fusion.4
  95.4 2.6 %select_add_fusion = s32[2048]{0:T(1024)S(1)} fusion(s32[2048]{0:T(1024)S(1)} %copy-done.6, s32[]{:T(128)} %get-tuple-element.27, s32[]{:T(128)} %get-tuple-element.25, s32[]{:T(128)} %get-tuple-element.26, s32[]{:T(128)} %get-tuple-element.24), kind=kLoop, calls=%fused_computation.34 | loop fusion | flops 22528 | bytes 16400 | tf_op jit(solution)/shard_map/add | solution.py:136
  98.0 0.4 copy.50.lo_ref
  98.4 0.0 all-gather.2.cloned.1.call-done
  98.4 3.1 %fusion.2 = bf16[2,2048,256]{1,2,0:T(8,128)(2,1)S(1)} fusion(bf16[2048,512]{1,0:T(8,128)(2,1)} %all-gather.2.cloned.1.call-done, bf16[1,4,512,256]{3,2,1,0:T(8,128)(2,1)} %param.9), kind=kOutput, calls=%fused_computation.5 | convolution fusion | flops 1074790400 | bytes 4718592 | tf_op jit(solution)/shard_map/tl,hlk->htk/dot_general | solution.py:144
  101.5 2.6 %copy.49 = bf16[2,2048,256]{2,1,0:T(8,128)(2,1)} copy(bf16[2,2048,256]{1,2,0:T(8,128)(2,1)S(1)} %fusion.2) | data formatting | bytes 4194304 | tf_op jit(solution)/shard_map/convert_element_type | solution.py:145
  104.1 24.1 %shard_map.85 = (bf16[8,2,256,128]{3,2,1,0:T(8,128)(2,1)S(1)}, bf16[2,32,64,256]{3,2,1,0:T(8,128)(2,1)S(1)}) custom-call(s32[128]{0:T(128)S(1)} %reshape.41.lists_ref, s32[8,4,256]{2,1,0:T(4,128)S(1)} %broadcast_add_fusion.kp_ref, s32[2048,1]{1,0:T(8,128)S(1)} %copy.50.lo_ref, bf16[8,2,2,256,128]{4,3,2,1,0:T(8,128)(2,1)} %copy-done.3, ...), custom_call_target="tpu_custom_call" | custom-call | flops 1342177280 | bytes 7340032 | tf_op jit(solution)/shard_map/pallas_call | solution.py:79
  128.1 0.0 copy-start.1
  128.1 1.0 copy-done.1
  129.1 12.9 %all-to-all-done.1.qg_ref = bf16[8,2,2,256,128]{4,3,2,1,0:T(8,128)(2,1)} async-done(((bf16[8,2,2,256,128]{4,3,2,1,0:T(8,128)(2,1)}), bf16[8,2,2,256,128]{4,3,2,1,0:T(8,128)(2,1)}, u32[]{:S(2)}, u32[]{:S(2)}) %all-to-all-start.1) | async-done | bytes 2097184 | tf_op jit(solution)/shard_map/all_to_all | solution.py:125
  142.0 4.2 %all-to-all-start.2 = ((bf16[8,2,256,128]{3,2,1,0:T(8,128)(2,1)}), bf16[8,2,256,128]{3,2,1,0:T(8,128)(2,1)}, u32[]{:S(2)}, u32[]{:S(2)}) async-start(bf16[8,2,256,128]{3,2,1,0:T(8,128)(2,1)} %copy-done.1), calls=%async_computation.2 | async-start | bytes 2097152 | tf_op jit(solution)/shard_map/all_to_all | solution.py:147
  146.2 0.2 reduce-scatter.4.cloned.1.call-start
  146.5 4.4 %fusion.3 = bf16[2,2048,256]{1,2,0:T(8,128)(2,1)} fusion(bf16[2048,512]{1,0:T(8,128)(2,1)} %all-gather.2.cloned.1.call-done, bf16[1,4,512,256]{3,2,1,0:T(8,128)(2,1)} %param.9), kind=kOutput, calls=%fused_computation.6 | convolution fusion | flops 1074790400 | bytes 4718592 | tf_op jit(solution)/shard_map/tl,hlk->htk/dot_general | solution.py:144
  150.9 3.9 %copy.54 = bf16[2,2048,256]{2,1,0:T(8,128)(2,1)} copy(bf16[2,2048,256]{1,2,0:T(8,128)(2,1)} %fusion.3) | data formatting | bytes 4194304 | tf_op jit(solution)/shard_map/convert_element_type | solution.py:145
  154.8 0.0 copy-start.5
  154.8 24.7 %shard_map.86 = (bf16[8,2,256,128]{3,2,1,0:T(8,128)(2,1)}, bf16[2,32,64,256]{3,2,1,0:T(8,128)(2,1)S(1)}) custom-call(s32[128]{0:T(128)S(1)} %reshape.41.lists_ref, s32[8,4,256]{2,1,0:T(4,128)S(1)} %broadcast_add_fusion.kp_ref, s32[2048,1]{1,0:T(8,128)S(1)} %copy.50.lo_ref, bf16[8,2,2,256,128]{4,3,2,1,0:T(8,128)(2,1)} %all-to-all-done.1.qg_ref, ...), custom_call_target="tpu_custom_call" | custom-call | flops 1342177280 | bytes 7340032 | tf_op jit(solution)/shard_map/pallas_call | solution.py:79
  179.6 0.0 copy-start
  179.6 0.0 copy-done.5
  179.6 1.3 fusion.18
  180.8 0.0 copy-done
  180.9 2.6 %fusion.1 = bf16[512,2048]{0,1:T(8,128)(2,1)} fusion(bf16[2,2048,256]{2,1,0:T(8,128)(2,1)S(1)} %bitcast.87, f32[2048,512,1]{1,0,2:T(8,128)S(1)} %fusion.18, bf16[1,4,512,256]{3,2,1,0:T(8,128)(2,1)S(1)} %copy-done.5), kind=kOutput, calls=%fused_computation.4 | convolution fusion | flops 1075838976 | bytes 8912896 | tf_op jit(solution)/shard_map/hlk,htk->lt/dot_general | solution.py:149
  183.5 0.0 all-to-all-done.2
  183.5 3.9 %copy.65 = bf16[512,2048]{1,0:T(8,128)(2,1)} copy(bf16[512,2048]{0,1:T(8,128)(2,1)} %fusion.1) | data formatting | bytes 4194304
  187.4 0.0 reduce-scatter.4.cloned.1.call-update
  187.4 5.7 %all-to-all-start.3 = ((bf16[8,2,256,128]{3,2,1,0:T(8,128)(2,1)}), bf16[8,2,256,128]{3,2,1,0:T(8,128)(2,1)S(1)}, u32[]{:S(2)}, u32[]{:S(2)}) async-start(bf16[8,2,256,128]{3,2,1,0:T(8,128)(2,1)} %get-tuple-element.13), calls=%async_computation.3 | async-start | bytes 2097152 | tf_op jit(solution)/shard_map/all_to_all | solution.py:147
  193.1 26.8 %reduce-scatter.4.cloned.1.call-done = bf16[128,2048]{1,0:T(8,128)(2,1)} async-done(((bf16[512,2048]{1,0:T(8,128)(2,1)}), bf16[128,2048]{1,0:T(8,128)(2,1)}) %reduce-scatter.4.cloned.1.call-update) | async-done | bytes 524304
  219.9 2.1 copy.66
  222.0 0.0 all-to-all-done.3
  222.0 5.5 %all-to-all-start.4 = ((bf16[8,256,128]{2,1,0:T(8,128)(2,1)}), bf16[8,256,128]{2,1,0:T(8,128)(2,1)}, u32[]{:S(2)}, u32[]{:S(2)}) async-start(bf16[8,256,128]{2,1,0:T(8,128)(2,1)} %bitcast.95), calls=%async_computation.4 | async-start | bytes 1048576 | tf_op jit(solution)/shard_map/all_to_all | solution.py:156
  227.5 0.0 copy-start.2
  227.5 3.6 %fusion.13 = f32[2,512,256]{1,2,0:T(8,128)S(1)} fusion(bf16[2,2048,256]{2,1,0:T(8,128)(2,1)} %bitcast.88, bf16[2048,512]{1,0:T(8,128)(2,1)} %all-gather.2.cloned.1.call-done), kind=kOutput, calls=%fused_computation.18 | convolution fusion | flops 1073741824 | bytes 5242880 | tf_op jit(solution)/shard_map/tl,htk->hlk/dot_general | solution.py:151
  231.2 0.0 copy-done.2
  231.2 1.3 fusion.10
  232.5 0.2 maximum_bitcast_fusion
  232.6 1.8 copy.60
  234.4 1.4 pad_maximum_fusion.2
  235.9 2.7 %copy.59 = bf16[256,32,128]{2,1,0:T(8,128)(2,1)} copy(bf16[256,32,128]{2,0,1:T(8,128)(2,1)S(1)} %bitcast.91) | data formatting | bytes 4194304
  238.5 3.6 %all-to-all-done.4 = bf16[8,256,128]{2,1,0:T(8,128)(2,1)} async-done(((bf16[8,256,128]{2,1,0:T(8,128)(2,1)}), bf16[8,256,128]{2,1,0:T(8,128)(2,1)}, u32[]{:S(2)}, u32[]{:S(2)}) %all-to-all-start.4) | async-done | bytes 524320 | tf_op jit(solution)/shard_map/all_to_all | solution.py:156
  242.1 1.8 convert_reduce_fusion
  (3 shorter events, 0.0 us)
Async XLA Ops:
  7.2 2.6 %copy-start.4 = (bf16[256,32,128]{2,1,0:T(8,128)(2,1)S(1)}, bf16[256,32,128]{2,1,0:T(8,128)(2,1)}, u32[]{:S(2)}) copy-start(bf16[256,32,128]{2,1,0:T(8,128)(2,1)} %param.7) | copy-start | bytes 6291460
  13.6 74.7 %all-to-all-start = ((bf16[8,2,2,256,128]{4,3,2,1,0:T(8,128)(2,1)}), bf16[8,2,2,256,128]{4,3,2,1,0:T(8,128)(2,1)S(1)}, u32[]{:S(2)}, u32[]{:S(2)}) async-start(bf16[8,2,2,256,128]{4,3,2,1,0:T(8,128)(2,1)} %copy.47), calls=%async_computation | async-start | bytes 4194304 | tf_op jit(solution)/shard_map/all_to_all | solution.py:125
  20.9 77.5 %all-gather.2.cloned.1.call-start = ((), (), s32[]{:S(2)}) async-start(), calls=%async_computation.6 | async-start | bytes 2359296 | tf_op jit(solution)/shard_map/all_gather | solution.py:116
  24.4 69.7 %copy-start.7 = (s32[32,4]{0,1:T(4,128)S(1)}, s32[32,4]{0,1:T(4,128)}, u32[]{:S(2)}) copy-start(s32[32,4]{0,1:T(4,128)} %param.11) | copy-start | bytes 1540
  24.4 70.3 %copy-start.6 = (s32[2048]{0:T(1024)S(1)}, s32[2048]{0:T(1024)}, u32[]{:S(2)}) copy-start(s32[2048]{0:T(1024)} %param.10) | copy-start | bytes 24580
  88.4 1.3 copy-start.3
  89.7 52.3 %all-to-all-start.1 = ((bf16[8,2,2,256,128]{4,3,2,1,0:T(8,128)(2,1)}), bf16[8,2,2,256,128]{4,3,2,1,0:T(8,128)(2,1)}, u32[]{:S(2)}, u32[]{:S(2)}) async-start(bf16[8,2,2,256,128]{4,3,2,1,0:T(8,128)(2,1)} %pad_maximum_fusion.1), calls=%async_computation.1 | async-start | bytes 4194304 | tf_op jit(solution)/shard_map/all_to_all | solution.py:125
  128.1 1.0 copy-start.1
  142.0 41.5 %all-to-all-start.2 = ((bf16[8,2,256,128]{3,2,1,0:T(8,128)(2,1)}), bf16[8,2,256,128]{3,2,1,0:T(8,128)(2,1)}, u32[]{:S(2)}, u32[]{:S(2)}) async-start(bf16[8,2,256,128]{3,2,1,0:T(8,128)(2,1)} %copy-done.1), calls=%async_computation.2 | async-start | bytes 2097152 | tf_op jit(solution)/shard_map/all_to_all | solution.py:147
  146.2 73.7 %reduce-scatter.4.cloned.1.call-start = ((), (), s32[]{:S(2)}) async-start(), calls=%async_computation.7 | async-start | bytes 2621440
  154.8 24.8 %copy-start.5 = (bf16[1,4,512,256]{3,2,1,0:T(8,128)(2,1)S(1)}, bf16[1,4,512,256]{3,2,1,0:T(8,128)(2,1)}, u32[]{:S(2)}) copy-start(bf16[1,4,512,256]{3,2,1,0:T(8,128)(2,1)} %param.9) | copy-start | bytes 3145732
  179.6 1.3 copy-start
  187.4 34.6 %all-to-all-start.3 = ((bf16[8,2,256,128]{3,2,1,0:T(8,128)(2,1)}), bf16[8,2,256,128]{3,2,1,0:T(8,128)(2,1)S(1)}, u32[]{:S(2)}, u32[]{:S(2)}) async-start(bf16[8,2,256,128]{3,2,1,0:T(8,128)(2,1)} %get-tuple-element.13), calls=%async_computation.3 | async-start | bytes 2097152 | tf_op jit(solution)/shard_map/all_to_all | solution.py:147
  222.0 20.1 %all-to-all-start.4 = ((bf16[8,256,128]{2,1,0:T(8,128)(2,1)}), bf16[8,256,128]{2,1,0:T(8,128)(2,1)}, u32[]{:S(2)}, u32[]{:S(2)}) async-start(bf16[8,256,128]{2,1,0:T(8,128)(2,1)} %bitcast.95), calls=%async_computation.4 | async-start | bytes 1048576 | tf_op jit(solution)/shard_map/all_to_all | solution.py:156
  227.5 3.6 %copy-start.2 = (bf16[2048,512]{1,0:T(8,128)(2,1)S(1)}, bf16[2048,512]{1,0:T(8,128)(2,1)}, u32[]{:S(2)}) copy-start(bf16[2048,512]{1,0:T(8,128)(2,1)} %all-gather.2.cloned.1.call-done) | copy-start | bytes 6291460
Sparse Core Ops, SparseCore 0:
  23.9 71.0 all-gather.1
  187.5 32.3 reduce-scatter.3
